TPU v7x, 256 devices: a whole 4x4x8 slice. The times are simulated.
256 devices in a mesh: ctx: 32 (over z, x_lo, core), head: 8 (over y, x_hi).
Axes of the slice: x: 4 (x_hi: 2, x_lo: 2; x = x_hi * 2 + x_lo), y: 4, z: 8, core: 2. Of those that a mesh axis runs over, the one named last changes fastest.
Arguments:
- query_rows: bfloat16 [4096, 32, 128], P('ctx', 'head'), may hold values from -6 to 6, as said below
- key_rows: bfloat16 [4096, 16, 128], P('ctx', 'head'), may hold values from -6 to 6, as said below
- value_rows: bfloat16 [4096, 16, 128], P('ctx', 'head'), may hold values from -6 to 6
- query_tangent: bfloat16 [4096, 32, 128], P('ctx', 'head'), may hold values from -6 to 6
- key_tangent: bfloat16 [4096, 16, 128], P('ctx', 'head'), may hold values from -6 to 6
- value_tangent: bfloat16 [4096, 16, 128], P('ctx', 'head'), may hold values from -6 to 6
- curvature: float32 [32, 4096], P('head', 'ctx'), may hold values from 0.5 to 8192, as said below
- documents: int32 [4096], P('ctx'), may hold values from 0 to 7, never falling along the last dimension, each value on 1 to 2048 neighbouring positions
Outputs:
- query_grad: bfloat16 [4096, 32, 128], P('ctx', 'head')
- key_grad: bfloat16 [4096, 16, 128], P('ctx', 'head')
- value_grad: bfloat16 [4096, 16, 128], P('ctx', 'head')
- doc_scores: float32 [8], replicated
Inputs may be any that keep to these rules, and one draw needn't show every extreme that they name: `query_rows`: finite entries. `key_rows`: finite entries. `curvature`: positive entries.
All inputs are finite; a program needn't handle non-finite values.
Results may differ from a plain program's by a relative error of at most 0.019.
Values may be sent and summed in bfloat16 or wider, within the bound.
No kernel may reach another device: no remote copies, remote signals or barrier semaphores. Data moves between devices by JAX's collectives and lax.ppermute only.
A program may use at most 64 MiB of HBM per device.

v0:
```python
from functools import partial
import math

import jax
import jax.numpy as jnp
from jax import lax
from jax.sharding import PartitionSpec as P

DOCS = 8


score_scale = 1.0 / 12.0
lowest_score = -1e30


def blockwise(row_count, update, carried):
    block_len = math.gcd(row_count, 512)

    def advance(counter, inner_state):
        return update(inner_state, counter * block_len, block_len)

    return lax.fori_loop(0, row_count // block_len, advance, carried)


def guarded(update, carried):
    result = update(carried)
    return result


def forward_update(context, pieces, first_row, offset, block_len, carried):
    queries, query_tan, positions = context
    key_block, value_block, key_tan, value_tan = [
        lax.dynamic_slice_in_dim(section, offset, block_len, 0) for section in pieces
    ]
    maxima, totals, spreads, outputs, tangents = carried
    scores = (
        jnp.einsum("tgpd,rgd->tgpr", queries, key_block, preferred_element_type=jnp.float32)
        * score_scale
    )
    slopes = (
        jnp.einsum("tgpd,rgd->tgpr", query_tan, key_block, preferred_element_type=jnp.float32)
        + jnp.einsum("tgpd,rgd->tgpr", queries, key_tan, preferred_element_type=jnp.float32)
    ) * score_scale
    columns = offset + lax.iota(jnp.int32, block_len)
    allowed = (columns[None, :] <= positions[:, None])[:, None, None, :]
    new_max = jnp.maximum(maxima, jnp.max(jnp.where(allowed, scores, lowest_score), axis=-1))
    factor = jnp.exp(maxima - new_max)
    weights = jnp.where(allowed, jnp.exp(scores - new_max[..., None]), 0.0)
    weighted = weights * slopes
    totals = totals * factor + jnp.sum(weights, axis=-1)
    spreads = spreads * factor + jnp.sum(weighted, axis=-1)
    weights_low = weights.astype(jnp.bfloat16)
    outputs = outputs * factor[..., None] + jnp.einsum(
        "tgpr,rgd->tgpd", weights_low, value_block, preferred_element_type=jnp.float32
    )
    tangents = (
        tangents * factor[..., None]
        + jnp.einsum(
            "tgpr,rgd->tgpd",
            weighted.astype(jnp.bfloat16),
            value_block,
            preferred_element_type=jnp.float32,
        )
        + jnp.einsum("tgpr,rgd->tgpd", weights_low, value_tan, preferred_element_type=jnp.float32)
    )
    return (new_max, totals, spreads, outputs, tangents)


def forward_fold(context, carried, pieces, first_row):

    def update(inner_state, offset, block_len):
        return guarded(
            partial(forward_update, context, pieces, first_row, offset, block_len), inner_state
        )

    return blockwise(pieces[0].shape[0], update, carried)


def backward_block(context, key_block, value_block, columns):
    queries, positions, cotangent, log_totals, deltas = context
    scores = (
        jnp.einsum("tgpd,rgd->tgpr", queries, key_block, preferred_element_type=jnp.float32)
        * score_scale
    )
    allowed = (columns[None, :] <= positions[:, None])[:, None, None, :]
    probability = jnp.where(allowed, jnp.exp(scores - log_totals[..., None]), 0.0)
    pushed = jnp.einsum(
        "tgpd,rgd->tgpr", cotangent, value_block, preferred_element_type=jnp.float32
    )
    grad_scores = probability * (pushed - deltas[..., None])
    return (probability, grad_scores)


def query_update(context, pieces, first_row, offset, block_len, carried):
    key_block, value_block = [
        lax.dynamic_slice_in_dim(section, offset, block_len, 0) for section in pieces
    ]
    columns = offset + lax.iota(jnp.int32, block_len)
    probability, grad_scores = backward_block(context, key_block, value_block, columns)
    return (
        carried
        + jnp.einsum(
            "tgpr,rgd->tgpd",
            grad_scores.astype(jnp.bfloat16),
            key_block,
            preferred_element_type=jnp.float32,
        )
        * score_scale
    )


def query_fold(context, carried, pieces, first_row):

    def update(inner_state, offset, block_len):
        return guarded(
            partial(query_update, context, pieces, first_row, offset, block_len), inner_state
        )

    return blockwise(pieces[0].shape[0], update, carried)


def key_update(context, pieces, first_row, offset, block_len, carried):
    key_block, value_block, positions = context
    part_q, part_cot, part_log, part_delta = [
        lax.dynamic_slice_in_dim(section, offset, block_len, 0) for section in pieces
    ]
    scores = (
        jnp.einsum("rgpd,tgd->tgpr", part_q, key_block, preferred_element_type=jnp.float32)
        * score_scale
    )
    columns = offset + lax.iota(jnp.int32, block_len)
    allowed = (columns[None, :] >= positions[:, None])[:, None, None, :]
    log_cols = jnp.transpose(part_log, (1, 2, 0))[None]
    delta_cols = jnp.transpose(part_delta, (1, 2, 0))[None]
    probability = jnp.where(allowed, jnp.exp(scores - log_cols), 0.0)
    pushed = jnp.einsum("rgpd,tgd->tgpr", part_cot, value_block, preferred_element_type=jnp.float32)
    grad_scores = probability * (pushed - delta_cols)
    key_grad, value_grad = carried
    key_grad = (
        key_grad
        + jnp.einsum(
            "tgpr,rgpd->tgd",
            grad_scores.astype(jnp.bfloat16),
            part_q,
            preferred_element_type=jnp.float32,
        )
        * score_scale
    )
    value_grad = value_grad + jnp.einsum(
        "tgpr,rgpd->tgd",
        probability.astype(jnp.bfloat16),
        part_cot,
        preferred_element_type=jnp.float32,
    )
    return (key_grad, value_grad)


def key_fold(context, carried, pieces, first_row):

    def update(inner_state, offset, block_len):
        return guarded(
            partial(key_update, context, pieces, first_row, offset, block_len), inner_state
        )

    return blockwise(pieces[0].shape[0], update, carried)


def on_device(
    query_rows,
    key_rows,
    value_rows,
    query_tangent,
    key_tangent,
    value_tangent,
    curvature,
    documents,
):
    tok_rows, head_count, head_width = query_rows.shape
    kv_groups = key_rows.shape[1]
    group_size = head_count // kv_groups
    first_pos = lax.axis_index("ctx") * tok_rows
    positions = first_pos + lax.iota(jnp.int32, tok_rows)
    queries = query_rows.reshape(tok_rows, kv_groups, group_size, head_width)
    query_tan = query_tangent.reshape(tok_rows, kv_groups, group_size, head_width)
    stat_shape = (tok_rows, kv_groups, group_size)
    zero_stats = jnp.zeros(stat_shape, jnp.float32)
    zero_rows = jnp.zeros(queries.shape, jnp.float32)
    start_state = (
        jnp.full(stat_shape, lowest_score, jnp.float32),
        zero_stats,
        zero_stats,
        zero_rows,
        zero_rows,
    )
    fwd_context = (queries, query_tan, positions)
    state = forward_fold(
        fwd_context,
        start_state,
        (
            lax.all_gather(key_rows, "ctx", axis=0, tiled=True),
            lax.all_gather(value_rows, "ctx", axis=0, tiled=True),
            lax.all_gather(key_tangent, "ctx", axis=0, tiled=True),
            lax.all_gather(value_tangent, "ctx", axis=0, tiled=True),
        ),
        jnp.int32(0),
    )
    maxima, totals, spreads, outputs, tangents = state
    outputs = outputs / totals[..., None]
    out_tan = tangents / totals[..., None] - (spreads / totals)[..., None] * outputs
    curv_rows = jnp.transpose(curvature).reshape(stat_shape)
    cotangent = (curv_rows[..., None] * out_tan).astype(jnp.bfloat16)
    log_totals = maxima + jnp.log(totals)
    deltas = jnp.sum(cotangent.astype(jnp.float32) * outputs, axis=-1)
    back_context = (queries, positions, cotangent, log_totals, deltas)
    query_grad = query_fold(
        back_context,
        zero_rows,
        (
            lax.all_gather(key_rows, "ctx", axis=0, tiled=True),
            lax.all_gather(value_rows, "ctx", axis=0, tiled=True),
        ),
        jnp.int32(0),
    )
    zero_keys = jnp.zeros(key_rows.shape, jnp.float32)
    key_grad, value_grad = key_fold(
        (key_rows, value_rows, positions),
        (zero_keys, zero_keys),
        (
            lax.all_gather(queries.astype(jnp.float32), "ctx", axis=0, tiled=True).astype(
                jnp.bfloat16
            ),
            lax.all_gather(cotangent.astype(jnp.float32), "ctx", axis=0, tiled=True).astype(
                jnp.bfloat16
            ),
            lax.all_gather(log_totals, "ctx", axis=0, tiled=True),
            lax.all_gather(deltas, "ctx", axis=0, tiled=True),
        ),
        jnp.int32(0),
    )
    token_terms = (
        jnp.sum(query_tan.astype(jnp.float32) * query_grad, axis=(1, 2, 3))
        + jnp.sum(key_tangent.astype(jnp.float32) * key_grad, axis=(1, 2))
        + jnp.sum(value_tangent.astype(jnp.float32) * value_grad, axis=(1, 2))
    )
    onehot = (documents[:, None] == lax.iota(jnp.int32, DOCS)[None, :]).astype(jnp.float32)
    doc_sums = jnp.dot(token_terms, onehot, precision=lax.Precision.HIGHEST)
    counts = jnp.sum(onehot, axis=0)
    doc_sums, counts = lax.psum((doc_sums, counts), ("ctx", "head"))
    doc_scores = doc_sums / (counts * (head_count * head_width))
    return (
        query_grad.reshape(tok_rows, head_count, head_width).astype(jnp.bfloat16),
        key_grad.astype(jnp.bfloat16),
        value_grad.astype(jnp.bfloat16),
        doc_scores,
    )


def solution(mesh):
    in_specs = (
        P("ctx", "head", None),
        P("ctx", "head", None),
        P("ctx", "head", None),
        P("ctx", "head", None),
        P("ctx", "head", None),
        P("ctx", "head", None),
        P("head", "ctx"),
        P("ctx"),
    )
    out_specs = (P("ctx", "head", None), P("ctx", "head", None), P("ctx", "head", None), P())
    return jax.shard_map(
        on_device, mesh=mesh, in_specs=in_specs, out_specs=out_specs, check_vma=False
    )
```

profile of v0, /device:TPU:8, one launch (start us, length us, event | category | flops | bytes accessed | tf_op | source)
XLA Modules:
  0.0 565.6 jit_solution(12759244747026467893)
XLA Ops:
  7.2 1.5 copy.65
  8.8 1.5 copy.68
  11.1 1.6 copy.69
  12.7 1.6 copy.66
  14.4 1.6 copy.101
  16.0 1.7 copy.67
  18.5 1.6 copy.80
  21.4 56.7 %all-gather.7.cloned.1.call-done = bf16[4096,2,128]{2,0,1:T(8,128)(2,1)} async-done(((bf16[128,2,128]{2,0,1:T(8,128)(2,1)}), bf16[4096,2,128]{2,0,1:T(8,128)(2,1)}) %all-gather.7.cloned.1.call-update) | async-done | bytes 2097168 | tf_op jit(solution)/shard_map/all_gather | solution.py:219
  78.1 66.9 %all-gather.9.cloned.1.call-done = bf16[4096,2,128]{2,0,1:T(8,128)(2,1)} async-done(((bf16[128,2,128]{2,0,1:T(8,128)(2,1)}), bf16[4096,2,128]{2,0,1:T(8,128)(2,1)}) %all-gather.9.cloned.1.call-update) | async-done | bytes 2097168 | tf_op jit(solution)/shard_map/all_gather | solution.py:202
  145.0 66.3 %all-gather.11.cloned.1.call-done = bf16[4096,2,128]{2,1,0:T(2,128)(2,1)} async-done(((bf16[128,2,128]{2,1,0:T(2,128)(2,1)}), bf16[4096,2,128]{2,1,0:T(2,128)(2,1)}) %all-gather.11.cloned.1.call-update) | async-done | bytes 2097168 | tf_op jit(solution)/shard_map/all_gather | solution.py:220
  211.3 67.3 %all-gather.13.cloned.1.call-done = bf16[4096,2,128]{0,2,1:T(8,128)(2,1)} async-done(((bf16[128,2,128]{0,2,1:T(8,128)(2,1)}), bf16[4096,2,128]{0,2,1:T(8,128)(2,1)}) %all-gather.13.cloned.1.call-update) | async-done | bytes 2097168 | tf_op jit(solution)/shard_map/all_gather | solution.py:203
  278.7 62.4 %while.52 = (s32[]{:T(128)}, f32[128,2,2]{0,2,1:T(2,128)S(1)}, f32[128,2,2]{0,2,1:T(2,128)S(1)}, f32[128,2,2]{0,2,1:T(2,128)S(1)}, f32[128,2,2,128]{0,3,2,1:T(8,...) while((s32[]{:T(128)}, f32[128,2,2]{0,2,1:T(2,128)S(1)}, ...), condition=%wide.region_4.5_spmd.clone, body=%wide.region_0.4_spmd.clone.sunk | while | flops 408162432 | bytes 16045393 | solution.py:22
  342.3 1.6 multiply_reduce_fusion.1
  344.0 33.7 %while.53 = (s32[]{:T(128)}, f32[128,2,2,128]{0,3,2,1:T(8,128)S(1)}, bf16[4096,2,128]{2,0,1:T(8,128)(2,1)}, bf16[128,2,2,128]{3,0,2,1:T(8,128)(2,1)}, f32[128,2,...) while((s32[]{:T(128)}, ...), condition=%wide.region_7.8_spmd.clone, body=%wide.region_6.7_spmd.clone.sunk | while | flops 203162240 | bytes 4859117 | solution.py:22
  346.7 1.5 fusion.152
  355.1 1.5 fusion.152
  359.3 1.5 fusion.152
  363.5 1.5 fusion.152
  371.9 1.5 fusion.152
  376.2 1.5 fusion.152
  378.5 32.8 %all_gather.31 = f32[4096,2,2]{0,2,1:T(2,128)S(1)} all-gather(f32[128,2,2]{0,2,1:T(2,128)S(1)} %get-tuple-element.1219), channel_id=1, replica_groups=mesh['ctx'=32,'head'=8] {'ctx'}, dimensions={0}, use_global_device_ids=true | all-gather | bytes 67584 | tf_op jit(solution)/shard_map/all_gather | solution.py:235
  411.3 30.8 %all_gather.33 = f32[4096,2,2]{0,2,1:T(2,128)S(1)} all-gather(f32[128,2,2]{0,2,1:T(2,128)S(1)} %get-tuple-element.1218), channel_id=1, replica_groups=mesh['ctx'=32,'head'=8] {'ctx'}, dimensions={0}, use_global_device_ids=true | all-gather | bytes 67584 | tf_op jit(solution)/shard_map/all_gather | solution.py:236
  442.2 40.0 %while.54 = (s32[]{:T(128)}, f32[128,2,128]{0,2,1:T(8,128)S(1)}, f32[128,2,128]{0,2,1:T(8,128)S(1)}, bf16[4096,2,2,128]{3,0,2,1:T(8,128)(2,1)}, bf16[128,2,128]{...) while((s32[]{:T(128)}, f32[128,2,128]{0,2,1:T(8,128)S(1)}, ...), condition=%wide.region_9.10_spmd.clone, body=%wide.region_8.9_spmd.clone.sunk | while | flops 270500480 | bytes 6085337 | solution.py:22
  443.9 1.9 fusion.161
  448.9 1.9 fusion.161
  453.9 1.9 fusion.161
  458.9 1.9 fusion.161
  463.9 1.9 fusion.161
  468.9 1.9 fusion.161
  473.9 1.9 fusion.161
  478.9 1.9 fusion.161
  484.0 74.3 %all-reduce = (f32[8]{0:T(128)S(1)}, f32[8]{0:T(128)S(1)}) all-reduce(f32[8]{0:T(128)S(1)} %convolution_bitcast_fusion.6, f32[8]{0:T(128)S(1)} %copy-done.11), channel_id=1, replica_groups=mesh['ctx'=32,'head'=8] {'ctx','head'}, use_global_device_ids=true, to_apply=%region_13.14 | all-reduce | flops 16 | bytes 128 | tf_op jit(solution)/shard_map/psum | solution.py:248
  (332 shorter events, 117.0 us)
Async XLA Ops:
  7.2 70.9 %all-gather.7.cloned.1.call-start = ((), (), s32[]{:S(2)}) async-start(), calls=%async_computation | async-start | bytes 2162688 | tf_op jit(solution)/shard_map/all_gather | solution.py:219
  8.7 136.3 %all-gather.9.cloned.1.call-start = ((), (), s32[]{:S(2)}) async-start(), calls=%async_computation.1 | async-start | bytes 2162688 | tf_op jit(solution)/shard_map/all_gather | solution.py:202
  10.3 201.1 %all-gather.11.cloned.1.call-start = ((), (), s32[]{:S(2)}) async-start(), calls=%async_computation.2 | async-start | bytes 2162688 | tf_op jit(solution)/shard_map/all_gather | solution.py:220
  11.0 267.7 %all-gather.13.cloned.1.call-start = ((), (), s32[]{:S(2)}) async-start(), calls=%async_computation.3 | async-start | bytes 2162688 | tf_op jit(solution)/shard_map/all_gather | solution.py:203
  12.7 429.5 %all-gather.15.cloned.1.call-start = ((), (), s32[]{:S(2)}) async-start(), calls=%async_computation.4 | async-start | bytes 4325376 | tf_op jit(solution)/shard_map/all_gather | solution.py:229
  14.3 427.9 %all-gather.17.cloned.1.call-start = ((), (), s32[]{:S(2)}) async-start(), calls=%async_computation.5 | async-start | bytes 4325376 | tf_op jit(solution)/shard_map/all_gather | solution.py:232
  278.7 2.8 copy-start
  286.4 2.8 copy-start
  294.2 2.8 copy-start
  302.0 2.8 copy-start
  306.3 1.6 copy-start.1
  309.8 2.9 copy-start
  317.6 2.8 copy-start
  325.4 2.9 copy-start
  333.2 2.9 copy-start
  337.5 1.6 copy-start.1
  343.9 33.7 %copy-start.7 = (bf16[128,4,128]{0,2,1:T(8,128)(2,1)S(1)}, bf16[128,4,128]{0,2,1:T(8,128)(2,1)}, u32[]{:S(2)}) copy-start(bf16[128,4,128]{0,2,1:T(8,128)(2,1)} %copy.67) | copy-start | bytes 393220
  343.9 98.3 %copy-start.3 = (f32[128,2,128]{0,2,1:T(8,128)S(1)}, f32[128,2,128]{0,2,1:T(8,128)}, u32[]{:S(2)}) copy-start(f32[128,2,128]{0,2,1:T(8,128)} %custom-call.6) | copy-start | bytes 393220
  343.9 98.2 %copy-start.4 = (f32[128,2,128]{0,2,1:T(8,128)S(1)}, f32[128,2,128]{0,2,1:T(8,128)}, u32[]{:S(2)}) copy-start(f32[128,2,128]{0,2,1:T(8,128)} %custom-call.7) | copy-start | bytes 393220
  343.9 98.2 %copy-start.8 = (bf16[128,2,128]{2,0,1:T(8,128)(2,1)S(1)}, bf16[128,2,128]{2,0,1:T(8,128)(2,1)}, u32[]{:S(2)}) copy-start(bf16[128,2,128]{2,0,1:T(8,128)(2,1)} %copy.65) | copy-start | bytes 196612
  344.0 2.7 copy-start.5
  348.2 2.7 copy-start.5
  352.4 2.7 copy-start.5
  356.6 2.7 copy-start.5
  360.8 2.7 copy-start.5
  365.0 2.7 copy-start.5
  369.2 2.7 copy-start.5
  373.5 2.7 copy-start.5
  442.2 40.8 %copy-start.6 = (bf16[128,2,128]{0,2,1:T(8,128)(2,1)S(1)}, bf16[128,2,128]{0,2,1:T(8,128)(2,1)}, u32[]{:S(2)}) copy-start(bf16[128,2,128]{0,2,1:T(8,128)(2,1)} %copy.69) | copy-start | bytes 196612
  442.2 40.8 %copy-start.9 = (bf16[128,2,128]{0,2,1:T(8,128)(2,1)S(1)}, bf16[128,2,128]{0,2,1:T(8,128)(2,1)}, u32[]{:S(2)}) copy-start(bf16[128,2,128]{0,2,1:T(8,128)(2,1)} %copy.80) | copy-start | bytes 196612
  442.2 40.9 %copy-start.10 = (s32[128]{0:T(128)S(1)}, s32[128]{0:T(128)}, u32[]{:S(2)}) copy-start(s32[128]{0:T(128)} %param.21) | copy-start | bytes 1540
  442.2 41.7 %copy-start.11 = (f32[8]{0:T(128)S(1)}, f32[8]{0:T(128)}, u32[]{:S(2)}) copy-start(f32[8]{0:T(128)} %convert_reduce_fusion) | copy-start | bytes 100
  (14 other events, 21.8 us)
Sparse Core Ops, SparseCore 0:
  10.4 67.6 all-gather.6
  80.5 64.4 all-gather.8
  146.9 64.3 all-gather.10
  213.0 65.6 all-gather.12
  280.4 65.0 all-gather.14
  347.2 66.5 all-gather.16
where the time goes:
time: 571 us; the launch traced here: 566 us
  waiting for transfers between devices  258 us (45%)
  blocking collectives  138 us (24%)
  matrix products  108 us (19%)
  local copies, waits for them, and re-layouts  35.2 us (6%)
  between operations  14.3 us (3%)
  other arithmetic  8.96 us (2%)
    psum x1, blocking collectives, on_device(): doc_sums, counts = lax.psum((doc_sums, counts), ('ctx', 'head'))  74.3 us
    all_gather x1, waiting for transfers between devices, on_device(): lax.all_gather(value_tangent, 'ctx', axis=0, tiled=True)  67.3 us
    all_gather x1, waiting for transfers between devices, on_device(): lax.all_gather(key_tangent, 'ctx', axis=0, tiled=True)  66.9 us
    all_gather x1, waiting for transfers between devices, on_device(): lax.all_gather(value_rows, 'ctx', axis=0, tiled=True)  66.3 us
    all_gather x1, waiting for transfers between devices, on_device(): lax.all_gather(key_rows, 'ctx', axis=0, tiled=True)  56.7 us
    all_gather x1, blocking collectives, on_device(): lax.all_gather(log_totals, 'ctx', axis=0, tiled=True)  32.8 us
    all_gather x1, blocking collectives, on_device(): lax.all_gather(deltas, 'ctx', axis=0, tiled=True)  30.8 us
    dot_general x8, matrix products, key_update(): jnp.einsum('tgpr,rgpd->tgd', grad_scores.astype(jnp.bfloat16), part_q, pr...  15.1 us
  transfers between devices with their start and end apart: 6, of which 4 were waited for; matrix products, arithmetic and copies ran while one was open for 19% of the time, Pallas kernels for 0%

commit v1 on v0

v1 whole, which is shorter than its diff:
```python
import jax
import jax.numpy as jnp
from jax import lax
from jax.experimental import pallas as pl
from jax.experimental.pallas import tpu as pltpu
from jax.sharding import Mesh, PartitionSpec as P

DOCS = 8
NZ = 8
ROWS = 128
HD = 128
CH = 2 * ROWS
MQ = 2 * CH
BK = 2 * CH
SCALE = 1.0 / 12.0
LOWEST = -1e30
ALL = ("z", "xl", "c", "h")
BF = jnp.bfloat16
F32 = jnp.float32


def dot_nt(a, b):
    return lax.dot_general(a, b, (((1,), (1,)), ((), ())), preferred_element_type=F32)


def dot_nn(a, b):
    return lax.dot_general(a, b, (((1,), (0,)), ((), ())), preferred_element_type=F32)


def dot_tn(a, b):
    return lax.dot_general(a, b, (((0,), (0,)), ((), ())), preferred_element_type=F32)


def attention_kernel(*refs):
    at_ref, q_ref, curv_ref = refs[:3]
    chunks = refs[3 : 3 + 2 * NZ]
    gq_ref, gkv_ref = refs[3 + 2 * NZ : 5 + 2 * NZ]
    kv, score, acc_v, acc_t, top, tot, spr, sems = refs[5 + 2 * NZ :]
    z = at_ref[0]
    core = at_ref[1]

    def copy_of(d, side):
        return pltpu.make_async_copy(
            chunks[side * NZ + d], kv.at[d, pl.ds(side * CH, CH)], sems.at[d, side]
        )

    for d in range(NZ):
        for side in range(2):
            copy_of(d, side).start()

    def wait_for(d):
        for side in range(2):
            pltpu.make_async_copy(
                kv.at[d, pl.ds(side * CH, CH)], kv.at[d, pl.ds(side * CH, CH)], sems.at[d, side]
            ).wait()

    def forward(d, diagonal):
        wait_for(d)
        s = dot_nt(q_ref[:, HD:], kv[d, :, :HD])
        slope = dot_nt(q_ref[...], kv[d, :, : 2 * HD])
        if diagonal:
            row = lax.broadcasted_iota(jnp.int32, (MQ, BK), 0) % CH
            col = lax.broadcasted_iota(jnp.int32, (MQ, BK), 1)
            row_pos = (row // ROWS) * CH + core * ROWS + row % ROWS
            col_core = jnp.where(col >= CH, 1 - core, core)
            col = col % CH
            col_pos = (col // ROWS) * CH + col_core * ROWS + col % ROWS
            s = jnp.where(col_pos <= row_pos, s, LOWEST)
        score[d] = s
        block_top = jnp.max(s, axis=1, keepdims=True)
        if diagonal:
            new_top = block_top
        else:
            new_top = jnp.maximum(top[...], block_top)
        e = jnp.exp((s - new_top) * SCALE)
        f = e * (slope * SCALE)
        part_v = dot_nn(e.astype(BF), kv[d, :, 2 * HD :])
        part_t = dot_nn(f.astype(BF), kv[d, :, 2 * HD : 3 * HD])
        sum_e = jnp.sum(e, axis=1, keepdims=True)
        sum_f = jnp.sum(f, axis=1, keepdims=True)
        if diagonal:
            acc_v[...] = part_v
            acc_t[...] = part_t
            tot[...] = sum_e
            spr[...] = sum_f
        else:
            factor = jnp.exp((top[...] - new_top) * SCALE)
            acc_v[...] = acc_v[...] * factor + part_v
            acc_t[...] = acc_t[...] * factor + part_t
            tot[...] = tot[...] * factor + sum_e
            spr[...] = spr[...] * factor + sum_f
        top[...] = new_top

    forward(0, True)

    @pl.loop(1, z + 1)
    def _(d):
        forward(d, False)

    @pl.loop(z + 1, NZ)
    def _(d):
        wait_for(d)

    inv = 1.0 / tot[...]
    out = acc_v[:, :HD] * inv
    out_tan = (acc_t[...] + acc_v[:, HD:]) * inv - (spr[...] * inv) * out
    cot = (curv_ref[...] * out_tan).astype(BF)
    log_tot = top[...] * SCALE + jnp.log(tot[...])
    delta = jnp.sum(cot.astype(F32) * out, axis=1, keepdims=True)
    acc_t[...] = jnp.zeros((MQ, HD), F32)

    @pl.loop(0, z + 1)
    def _(d):
        p = jnp.exp(score[d] * SCALE - log_tot)
        g = p * (dot_nt(cot, kv[d, :, 2 * HD : 3 * HD]) - delta)
        gb = g.astype(BF)
        acc_t[...] += dot_nn(gb, kv[d, :, :HD])
        gkv_ref[d, :, :HD] = (dot_tn(gb, q_ref[:, HD:]) * SCALE).astype(BF)
        gkv_ref[d, :, HD:] = dot_tn(p.astype(BF), cot).astype(BF)

    @pl.loop(z + 1, NZ)
    def _(d):
        gkv_ref[d] = jnp.zeros((BK, 2 * HD), BF)

    gq_ref[...] = (acc_t[...] * SCALE).astype(BF)


def attention(at, q, curv, chunks):
    vmem = pl.BlockSpec(memory_space=pltpu.VMEM)
    return pl.pallas_call(
        attention_kernel,
        out_shape=(
            jax.ShapeDtypeStruct((MQ, HD), BF),
            jax.ShapeDtypeStruct((NZ, BK, 2 * HD), BF),
        ),
        in_specs=[pl.BlockSpec(memory_space=pltpu.SMEM), vmem, vmem]
        + [pl.BlockSpec(memory_space=pl.ANY)] * (2 * NZ),
        out_specs=(vmem, vmem),
        scratch_shapes=[
            pltpu.VMEM((NZ, BK, 4 * HD), BF),
            pltpu.VMEM((NZ, MQ, BK), F32),
            pltpu.VMEM((MQ, 2 * HD), F32),
            pltpu.VMEM((MQ, HD), F32),
            pltpu.VMEM((MQ, 1), F32),
            pltpu.VMEM((MQ, 1), F32),
            pltpu.VMEM((MQ, 1), F32),
            pltpu.SemaphoreType.DMA((NZ, 2)),
        ],
        compiler_params=pltpu.CompilerParams(vmem_limit_bytes=48 * 1024 * 1024),
        cost_estimate=pl.CostEstimate(
            flops=8 * 2 * MQ * 4096 * 256, bytes_accessed=8 << 20, transcendentals=2 * MQ * 4096
        ),
    )(at, q, curv, *chunks)


def swap(x, axis):
    return lax.ppermute(x, axis, [(0, 1), (1, 0)])


def around(x, step):
    return lax.ppermute(x, "z", [(i, (i + step) % NZ) for i in range(NZ)])


def pick(x, index, axis):
    return lax.dynamic_index_in_dim(x, index, axis, keepdims=False)


def on_device(
    query_rows,
    key_rows,
    value_rows,
    query_tangent,
    key_tangent,
    value_tangent,
    curvature,
    documents,
):
    z = lax.axis_index("z")
    xl = lax.axis_index("xl")
    core = lax.axis_index("c")
    kv_all = jnp.concatenate([key_rows, key_tangent, value_rows, value_tangent], axis=-1)
    q_all = jnp.concatenate([query_tangent, query_rows], axis=-1).reshape(ROWS, 2, 4 * HD)
    curv_all = curvature.reshape(2, 2, ROWS)
    both = jnp.concatenate([kv_all, q_all], axis=0)
    mine = pick(both, xl, 1)
    other = swap(pick(both, 1 - xl, 1), "xl")
    curv_mine = pick(curv_all, xl, 0)
    curv_other = swap(pick(curv_all, 1 - xl, 0), "xl")

    def ordered(a, b):
        return jnp.where(xl == 0, a, b), jnp.where(xl == 0, b, a)

    low, high = ordered(mine, other)
    chunk = jnp.concatenate([low[:ROWS], high[:ROWS]], axis=0)
    q = jnp.concatenate([low[ROWS:], high[ROWS:]], axis=0)
    q = jnp.concatenate([q[:, : 2 * HD], q[:, 2 * HD :]], axis=0)
    low_c, high_c = ordered(curv_mine, curv_other)
    curv = jnp.concatenate([low_c, high_c], axis=1).reshape(MQ, 1)

    chunks = [None] * NZ
    chunks[0] = chunk
    ahead = behind = chunk
    for step in range(1, NZ // 2):
        ahead = around(ahead, 1)
        behind = around(behind, -1)
        chunks[step] = ahead
        chunks[NZ - step] = behind
    chunks[NZ // 2] = jnp.concatenate([around(ahead[:ROWS], 1), around(behind[ROWS:], -1)], axis=0)
    sibling = [swap(c, "c") for c in chunks]

    at = jnp.stack([z, core])
    gq, gkv = attention(at, q, curv, chunks + sibling)

    gq = gq.reshape(2, 2, ROWS, HD)
    gq_other = swap(pick(gq, 1 - xl, 1), "xl")
    gq_mine = pick(gq, xl, 1)
    gq_low, gq_high = ordered(gq_mine, gq_other)
    query_grad = jnp.transpose(jnp.concatenate([gq_low, gq_high], axis=0), (1, 0, 2))

    from_sibling = swap(gkv[:, CH:], "c")
    part = (gkv[:, :CH].astype(F32) + from_sibling.astype(F32)).astype(BF)
    target = lax.rem(z - lax.iota(jnp.int32, NZ) + NZ, NZ)
    part = jnp.take(part, target, axis=0)
    part = part.reshape(2 * NZ * ROWS, 2 * HD)
    part = lax.all_to_all(part, ("z", "xl"), 0, 0, tiled=True)
    grads = jnp.sum(part.reshape(NZ, 2, ROWS, 2 * HD).astype(F32), axis=0)
    grads = jnp.transpose(grads, (1, 0, 2))
    key_grad = grads[..., :HD]
    value_grad = grads[..., HD:]

    token_terms = (
        jnp.sum(query_tangent.astype(F32) * query_grad.astype(F32), axis=(1, 2))
        + jnp.sum(key_tangent.astype(F32) * key_grad, axis=(1, 2))
        + jnp.sum(value_tangent.astype(F32) * value_grad, axis=(1, 2))
    )
    onehot = (documents[:, None] == lax.iota(jnp.int32, DOCS)[None, :]).astype(F32)
    doc_sums = jnp.sum(token_terms[:, None] * onehot, axis=0)
    counts = jnp.sum(onehot, axis=0)
    terms = jnp.concatenate([doc_sums, counts])
    world = NZ * 2 * 2 * 8
    spread = lax.all_to_all(jnp.tile(terms, world), ALL, 0, 0, tiled=True)
    doc_sums, counts = jnp.split(jnp.sum(spread.reshape(world, 2 * DOCS), axis=0), 2)
    doc_scores = doc_sums / (counts * (4 * HD))
    return (query_grad, key_grad.astype(BF), value_grad.astype(BF), doc_scores)


def solution(mesh):
    split = Mesh(mesh.devices.reshape(NZ, 2, 2, 8), ALL)
    ctx = ("z", "xl", "c")
    rows = P(ctx, "h", None)
    in_specs = (rows,) * 6 + (P("h", ctx), P(ctx))
    out_specs = (rows, rows, rows, P())
    return jax.shard_map(
        on_device, mesh=split, in_specs=in_specs, out_specs=out_specs, check_vma=False
    )
```

time: 571 us -> 140 us (0.25)
  the two profiles are of different devices: /device:TPU:8 before, /device:TPU:1 now
where the time goes in v1:
time: 140 us; the launch traced here: 139 us
  starting transfers between devices  60.4 us (43%)
  waiting for transfers between devices  53.7 us (38%)
  local copies, waits for them, and re-layouts  11.5 us (8%)
  other arithmetic  7.57 us (5%)
  Pallas kernels  4.72 us (3%)
    all_to_all x1, waiting for transfers between devices, on_device(): part = lax.all_to_all(part, ('z', 'xl'), 0, 0, tiled=True)  19.5 us
    all_to_all x1, starting transfers between devices, on_device(): part = lax.all_to_all(part, ('z', 'xl'), 0, 0, tiled=True)  19.5 us
    ppermute x8, starting transfers between devices, around(): return lax.ppermute(x, 'z', [(i, (i + step) % NZ) for i in range(NZ)])  15.2 us
    ppermute x12, starting transfers between devices, swap(): return lax.ppermute(x, axis, [(0, 1), (1, 0)])  13.8 us
    ppermute x8, waiting for transfers between devices, around(): return lax.ppermute(x, 'z', [(i, (i + step) % NZ) for i in range(NZ)])  12.7 us
    all_to_all x1, starting transfers between devices, on_device(): spread = lax.all_to_all(jnp.tile(terms, world), ALL, 0, 0, tiled=True)  12 us
    all_to_all x1, waiting for transfers between devices, on_device(): spread = lax.all_to_all(jnp.tile(terms, world), ALL, 0, 0, tiled=True)  11.6 us
    ppermute x12, waiting for transfers between devices, swap(): return lax.ppermute(x, axis, [(0, 1), (1, 0)])  9.85 us
  transfers between devices with their start and end apart: 22, of which 8 were waited for; matrix products, arithmetic and copies ran while one was open for 4% of the time, Pallas kernels for 0%

profile of v1, /device:TPU:1, one launch (start us, length us, event | category | flops | bytes accessed | tf_op | source)
XLA Modules:
  0.0 138.9 jit_solution(12033670746282161870)
XLA Ops:
  0.6 1.0 copy.51
  1.7 1.0 copy.52
  2.7 1.0 copy.47
  3.7 1.0 copy.48
  4.7 1.0 copy.49
  5.6 1.0 copy.50
  6.9 2.1 %collective-permute-start = (bf16[256,512]{1,0:T(8,128)(2,1)S(1)}, bf16[256,512]{1,0:T(8,128)(2,1)S(1)}, u32[]{:S(2)}, u32[]{:S(2)}) collective-permute-start(bf16[256,512]{1,0:T(8,128)(2,1)S(1)} %bitcast.44), channel_id=1, source_target_pairs={{0,16},{16,0},{1,17},{17,1},{2,18},{18,2},{3,19},{19,3},{4,20},{20... | collective-permute-start | bytes 786440 | tf_op jit(solution)/shard_map/ppermute | solution.py:157
  9.2 4.5 %collective-permute-done = bf16[256,512]{1,0:T(8,128)(2,1)S(1)} collective-permute-done((bf16[256,512]{1,0:T(8,128)(2,1)S(1)}, bf16[256,512]{1,0:T(8,128)(2,1)S(1)}, u32[]{:S(2)}, u32[]{:S(2)}) %collective-permute-start) | collective-permute-done | bytes 262176 | tf_op jit(solution)/shard_map/ppermute | solution.py:157
  14.5 3.0 %collective-permute-start.2 = (bf16[256,512]{1,0:T(8,128)(2,1)S(1)}, bf16[256,512]{1,0:T(8,128)(2,1)S(1)}, u32[]{:S(2)}, u32[]{:S(2)}) collective-permute-start(bf16[256,512]{1,0:T(8,128)(2,1)S(1)} %pad_maximum_fusion.3.refs_3_), channel_id=1, source_target_pairs={{0,32},{32,64},{64,96},{96,128},{128,160},{160,192},{192,224},{224... | collective-permute-start | bytes 786440 | tf_op jit(solution)/shard_map/ppermute | solution.py:161
  17.5 4.0 %collective-permute-start.6 = (bf16[256,512]{1,0:T(8,128)(2,1)S(1)}, bf16[256,512]{1,0:T(8,128)(2,1)S(1)}, u32[]{:S(2)}, u32[]{:S(2)}) collective-permute-start(bf16[256,512]{1,0:T(8,128)(2,1)S(1)} %pad_maximum_fusion.3.refs_3_), channel_id=1, source_target_pairs={{0,224},{32,0},{64,32},{96,64},{128,96},{160,128},{192,160},{224,1... | collective-permute-start | bytes 786440 | tf_op jit(solution)/shard_map/ppermute | solution.py:161
  21.5 5.0 %collective-permute-done.2.refs_4_ = bf16[256,512]{1,0:T(8,128)(2,1)S(1)} collective-permute-done((bf16[256,512]{1,0:T(8,128)(2,1)S(1)}, bf16[256,512]{1,0:T(8,128)(2,1)S(1)}, u32[]{:S(2)}, u32[]{:S(2)}) %collective-permute-start.2) | collective-permute-done | bytes 262176 | tf_op jit(solution)/shard_map/ppermute | solution.py:161
  26.5 2.7 %collective-permute-start.7 = (bf16[256,512]{1,0:T(8,128)(2,1)S(1)}, bf16[256,512]{1,0:T(8,128)(2,1)S(1)}, u32[]{:S(2)}, u32[]{:S(2)}) collective-permute-start(bf16[256,512]{1,0:T(8,128)(2,1)S(1)} %collective-permute-done.6.refs_10_), channel_id=1, source_target_pairs={{0,224},{32,0},{64,32},{96,64},{128,96},{160,128},{192,160},{224,1... | collective-permute-start | bytes 786440 | tf_op jit(solution)/shard_map/ppermute | solution.py:161
  29.2 4.1 %collective-permute-done.3.refs_5_ = bf16[256,512]{1,0:T(8,128)(2,1)S(1)} collective-permute-done((bf16[256,512]{1,0:T(8,128)(2,1)S(1)}, bf16[256,512]{1,0:T(8,128)(2,1)S(1)}, u32[]{:S(2)}, u32[]{:S(2)}) %collective-permute-start.3) | collective-permute-done | bytes 262176 | tf_op jit(solution)/shard_map/ppermute | solution.py:161
  33.3 2.7 %collective-permute-start.8 = (bf16[256,512]{1,0:T(8,128)(2,1)S(1)}, bf16[256,512]{1,0:T(8,128)(2,1)S(1)}, u32[]{:S(2)}, u32[]{:S(2)}) collective-permute-start(bf16[256,512]{1,0:T(8,128)(2,1)S(1)} %collective-permute-done.7.refs_9_), channel_id=1, source_target_pairs={{0,224},{32,0},{64,32},{96,64},{128,96},{160,128},{192,160},{224,1... | collective-permute-start | bytes 786440 | tf_op jit(solution)/shard_map/ppermute | solution.py:161
  36.0 1.2 collective-permute-start.1
  37.3 4.0 %collective-permute-start.10 = (bf16[256,512]{1,0:T(8,128)(2,1)S(1)}, bf16[256,512]{1,0:T(8,128)(2,1)S(1)}, u32[]{:S(2)}, u32[]{:S(2)}) collective-permute-start(bf16[256,512]{1,0:T(8,128)(2,1)S(1)} %pad_maximum_fusion.3.refs_3_), channel_id=1, source_target_pairs={{0,8},{8,0},{1,9},{9,1},{2,10},{10,2},{3,11},{11,3},{4,12},{12,4},... | collective-permute-start | bytes 786440 | tf_op jit(solution)/shard_map/ppermute | solution.py:157
  41.3 2.7 %collective-permute-start.17 = (bf16[256,512]{1,0:T(8,128)(2,1)S(1)}, bf16[256,512]{1,0:T(8,128)(2,1)S(1)}, u32[]{:S(2)}, u32[]{:S(2)}) collective-permute-start(bf16[256,512]{1,0:T(8,128)(2,1)S(1)} %collective-permute-done.6.refs_10_), channel_id=1, source_target_pairs={{0,8},{8,0},{1,9},{9,1},{2,10},{10,2},{3,11},{11,3},{4,12},{12,4},... | collective-permute-start | bytes 786440 | tf_op jit(solution)/shard_map/ppermute | solution.py:157
  44.1 2.7 %collective-permute-start.9 = (bf16[128,512]{1,0:T(8,128)(2,1)S(1)}, bf16[128,512]{1,0:T(8,128)(2,1)S(1)}, u32[]{:S(2)}, u32[]{:S(2)}) collective-permute-start(bf16[128,512]{1,0:T(8,128)(2,1)S(1)} %slice.57), channel_id=1, source_target_pairs={{0,224},{32,0},{64,32},{96,64},{128,96},{160,128},{192,160},{224,1... | collective-permute-start | bytes 393224 | tf_op jit(solution)/shard_map/ppermute | solution.py:161
  46.9 3.6 %collective-permute-done.5 = bf16[128,512]{1,0:T(8,128)(2,1)S(1)} collective-permute-done((bf16[128,512]{1,0:T(8,128)(2,1)S(1)}, bf16[128,512]{1,0:T(8,128)(2,1)S(1)}, u32[]{:S(2)}, u32[]{:S(2)}) %collective-permute-start.5) | collective-permute-done | bytes 131104 | tf_op jit(solution)/shard_map/ppermute | solution.py:161
  53.5 0.9 fusion.refs_1_
  54.4 4.7 %shard_map.111 = (bf16[512,128]{1,0:T(8,128)(2,1)S(1)}, bf16[8,512,256]{2,1,0:T(8,128)(2,1)}) custom-call(s32[2]{0:T(128)S(1)} %pad_add_fusion.refs_0_, bf16[512,256]{1,0:T(8,128)(2,1)S(1)} %fusion.refs_1_, f32[512,1]{1,0:T(8,128)S(1)} %bitcast.37, bf16[256,512]{1,0:T(8,128)(2,1)S(1)} %pad_maximum_fusion.3.refs_3_, ...), custom_call_target="tpu_custom_call" | custom-call | flops 8589934592 | bytes 8388608 | tf_op jit(solution)/shard_map/pallas_call | solution.py:130
  59.1 1.3 slice.45
  61.0 2.2 %collective-permute-done.19 = bf16[8,256,256]{2,1,0:T(8,128)(2,1)S(1)} collective-permute-done((bf16[8,256,256]{2,1,0:T(8,128)(2,1)S(1)}, bf16[8,256,256]{2,1,0:T(8,128)(2,1)S(1)}, u32[]{:S(2)}, u32[]{:S(2)}) %collective-permute-start.19) | collective-permute-done | bytes 1048608 | tf_op jit(solution)/shard_map/ppermute | solution.py:157
  63.2 1.5 %add_convert_fusion = bf16[8,256,256]{2,1,0:T(8,128)(2,1)S(1)} fusion(bf16[8,256,256]{2,1,0:T(8,128)(2,1)S(1)} %collective-permute-done.19, bf16[8,512,256]{2,1,0:T(8,128)(2,1)} %get-tuple-element.7), kind=kLoop, calls=%fused_computation.2 | loop fusion | flops 2097152 | bytes 3145728 | tf_op jit(solution)/shard_map/convert_element_type | solution.py:221
  65.3 1.1 broadcast_select_fusion
  66.5 19.5 %all-to-all-start = ((bf16[16,128,256]{2,1,0:T(8,128)(2,1)}), bf16[16,128,256]{2,1,0:T(8,128)(2,1)S(1)}, u32[]{:S(2)}, u32[]{:S(2)}) async-start(bf16[16,128,256]{2,1,0:T(8,128)(2,1)} %broadcast_select_fusion), calls=%async_computation | async-start | bytes 2097152 | tf_op jit(solution)/shard_map/all_to_all | solution.py:225
  86.0 1.4 %collective-permute-start.18 = (bf16[2,128,128]{2,0,1:T(2,128)(2,1)S(1)}, bf16[2,128,128]{2,0,1:T(2,128)(2,1)S(1)}, u32[]{:S(2)}, u32[]{:S(2)}) collective-permute-start(bf16[2,128,128]{2,0,1:T(2,128)(2,1)S(1)} %bitcast.45), channel_id=1, source_target_pairs={{0,16},{16,0},{1,17},{17,1},{2,18},{18,2},{3,19},{19,3},{4,20},{20... | collective-permute-start | bytes 196616 | tf_op jit(solution)/shard_map/ppermute | solution.py:157
  87.5 3.1 %collective-permute-done.18 = bf16[2,128,128]{2,0,1:T(2,128)(2,1)S(1)} collective-permute-done((bf16[2,128,128]{2,0,1:T(2,128)(2,1)S(1)}, bf16[2,128,128]{2,0,1:T(2,128)(2,1)S(1)}, u32[]{:S(2)}, u32[]{:S(2)}) %collective-permute-start.18) | collective-permute-done | bytes 65568 | tf_op jit(solution)/shard_map/ppermute | solution.py:157
  90.7 1.5 %multiply_reduce_fusion = (f32[128]{0:T(128)S(1)}, bf16[128,4,128]{2,1,0:T(4,128)(2,1)}) fusion(bf16[128,4,128]{2,1,0:T(4,128)(2,1)S(1)} %copy-done, bf16[2,128,128]{2,0,1:T(2,128)(2,1)S(1)} %get-tuple-element.33, bf16[2,128,128]{2,0,1:T(2,128)(2,1)S(1)} %get-tuple-element.32), kind=kLoop, calls=%fused_computation.13 | loop fusion | flops 524160 | bytes 393728 | tf_op jit(solution)/shard_map/reduce_sum | solution.py:232
  92.2 19.5 %all-to-all-done = bf16[16,128,256]{2,1,0:T(8,128)(2,1)S(1)} async-done(((bf16[16,128,256]{2,1,0:T(8,128)(2,1)}), bf16[16,128,256]{2,1,0:T(8,128)(2,1)S(1)}, u32[]{:S(2)}, u32[]{:S(2)}) %all-to-all-start) | async-done | bytes 1048608 | tf_op jit(solution)/shard_map/all_to_all | solution.py:225
  113.0 12.0 %all-to-all-start.1 = ((f32[256,16,1]{1,2,0:T(1,128)}), f32[256,16,1]{1,2,0:T(1,128)S(1)}, u32[]{:S(2)}, u32[]{:S(2)}) async-start(f32[256,16,1]{1,2,0:T(1,128)} %all_to_all.11), calls=%async_computation.1 | async-start | bytes 262144 | tf_op jit(solution)/shard_map/all_to_all | solution.py:241
  126.4 11.6 %all-to-all-done.1 = f32[256,16,1]{1,2,0:T(1,128)S(1)} async-done(((f32[256,16,1]{1,2,0:T(1,128)}), f32[256,16,1]{1,2,0:T(1,128)S(1)}, u32[]{:S(2)}, u32[]{:S(2)}) %all-to-all-start.1) | async-done | bytes 16416 | tf_op jit(solution)/shard_map/all_to_all | solution.py:241
  (73 shorter events, 9.4 us)
Async XLA Ops:
  6.7 29.2 %copy-start.3 = (f32[4,128]{1,0:T(4,128)S(1)}, f32[4,128]{1,0:T(4,128)}, u32[]{:S(2)}) copy-start(f32[4,128]{1,0:T(4,128)} %param.14) | copy-start | bytes 6148
  6.9 6.8 %collective-permute-start = (bf16[256,512]{1,0:T(8,128)(2,1)S(1)}, bf16[256,512]{1,0:T(8,128)(2,1)S(1)}, u32[]{:S(2)}, u32[]{:S(2)}) collective-permute-start(bf16[256,512]{1,0:T(8,128)(2,1)S(1)} %bitcast.44), channel_id=1, source_target_pairs={{0,16},{16,0},{1,17},{17,1},{2,18},{18,2},{3,19},{19,3},{4,20},{20... | collective-permute-start | bytes 786440 | tf_op jit(solution)/shard_map/ppermute | solution.py:157
  14.5 12.0 %collective-permute-start.2 = (bf16[256,512]{1,0:T(8,128)(2,1)S(1)}, bf16[256,512]{1,0:T(8,128)(2,1)S(1)}, u32[]{:S(2)}, u32[]{:S(2)}) collective-permute-start(bf16[256,512]{1,0:T(8,128)(2,1)S(1)} %pad_maximum_fusion.3.refs_3_), channel_id=1, source_target_pairs={{0,32},{32,64},{64,96},{96,128},{128,160},{160,192},{192,224},{224... | collective-permute-start | bytes 786440 | tf_op jit(solution)/shard_map/ppermute | solution.py:161
  17.5 9.0 %collective-permute-start.6 = (bf16[256,512]{1,0:T(8,128)(2,1)S(1)}, bf16[256,512]{1,0:T(8,128)(2,1)S(1)}, u32[]{:S(2)}, u32[]{:S(2)}) collective-permute-start(bf16[256,512]{1,0:T(8,128)(2,1)S(1)} %pad_maximum_fusion.3.refs_3_), channel_id=1, source_target_pairs={{0,224},{32,0},{64,32},{96,64},{128,96},{160,128},{192,160},{224,1... | collective-permute-start | bytes 786440 | tf_op jit(solution)/shard_map/ppermute | solution.py:161
  26.5 6.8 %collective-permute-start.3 = (bf16[256,512]{1,0:T(8,128)(2,1)S(1)}, bf16[256,512]{1,0:T(8,128)(2,1)S(1)}, u32[]{:S(2)}, u32[]{:S(2)}) collective-permute-start(bf16[256,512]{1,0:T(8,128)(2,1)S(1)} %collective-permute-done.2.refs_4_), channel_id=1, source_target_pairs={{0,32},{32,64},{64,96},{96,128},{128,160},{160,192},{192,224},{224... | collective-permute-start | bytes 786440 | tf_op jit(solution)/shard_map/ppermute | solution.py:161
  26.5 6.8 %collective-permute-start.7 = (bf16[256,512]{1,0:T(8,128)(2,1)S(1)}, bf16[256,512]{1,0:T(8,128)(2,1)S(1)}, u32[]{:S(2)}, u32[]{:S(2)}) collective-permute-start(bf16[256,512]{1,0:T(8,128)(2,1)S(1)} %collective-permute-done.6.refs_10_), channel_id=1, source_target_pairs={{0,224},{32,0},{64,32},{96,64},{128,96},{160,128},{192,160},{224,1... | collective-permute-start | bytes 786440 | tf_op jit(solution)/shard_map/ppermute | solution.py:161
  33.3 8.0 %collective-permute-start.4 = (bf16[256,512]{1,0:T(8,128)(2,1)S(1)}, bf16[256,512]{1,0:T(8,128)(2,1)S(1)}, u32[]{:S(2)}, u32[]{:S(2)}) collective-permute-start(bf16[256,512]{1,0:T(8,128)(2,1)S(1)} %collective-permute-done.3.refs_5_), channel_id=1, source_target_pairs={{0,32},{32,64},{64,96},{96,128},{128,160},{160,192},{192,224},{224... | collective-permute-start | bytes 786440 | tf_op jit(solution)/shard_map/ppermute | solution.py:161
  33.3 10.7 %collective-permute-start.8 = (bf16[256,512]{1,0:T(8,128)(2,1)S(1)}, bf16[256,512]{1,0:T(8,128)(2,1)S(1)}, u32[]{:S(2)}, u32[]{:S(2)}) collective-permute-start(bf16[256,512]{1,0:T(8,128)(2,1)S(1)} %collective-permute-done.7.refs_9_), channel_id=1, source_target_pairs={{0,224},{32,0},{64,32},{96,64},{128,96},{160,128},{192,160},{224,1... | collective-permute-start | bytes 786440 | tf_op jit(solution)/shard_map/ppermute | solution.py:161
  36.0 8.1 %collective-permute-start.1 = (f32[2,128]{1,0:T(2,128)S(1)}, f32[2,128]{1,0:T(2,128)S(1)}, u32[]{:S(2)}, u32[]{:S(2)}) collective-permute-start(f32[2,128]{1,0:T(2,128)S(1)} %fusion.3), channel_id=1, source_target_pairs={{0,16},{16,0},{1,17},{17,1},{2,18},{18,2},{3,19},{19,3},{4,20},{20... | collective-permute-start | bytes 3080 | tf_op jit(solution)/shard_map/ppermute | solution.py:157
  37.3 14.1 %collective-permute-start.10 = (bf16[256,512]{1,0:T(8,128)(2,1)S(1)}, bf16[256,512]{1,0:T(8,128)(2,1)S(1)}, u32[]{:S(2)}, u32[]{:S(2)}) collective-permute-start(bf16[256,512]{1,0:T(8,128)(2,1)S(1)} %pad_maximum_fusion.3.refs_3_), channel_id=1, source_target_pairs={{0,8},{8,0},{1,9},{9,1},{2,10},{10,2},{3,11},{11,3},{4,12},{12,4},... | collective-permute-start | bytes 786440 | tf_op jit(solution)/shard_map/ppermute | solution.py:157
  41.2 10.7 %collective-permute-start.11 = (bf16[256,512]{1,0:T(8,128)(2,1)S(1)}, bf16[256,512]{1,0:T(8,128)(2,1)S(1)}, u32[]{:S(2)}, u32[]{:S(2)}) collective-permute-start(bf16[256,512]{1,0:T(8,128)(2,1)S(1)} %collective-permute-done.2.refs_4_), channel_id=1, source_target_pairs={{0,8},{8,0},{1,9},{9,1},{2,10},{10,2},{3,11},{11,3},{4,12},{12,4},... | collective-permute-start | bytes 786440 | tf_op jit(solution)/shard_map/ppermute | solution.py:157
  41.3 10.7 %collective-permute-start.17 = (bf16[256,512]{1,0:T(8,128)(2,1)S(1)}, bf16[256,512]{1,0:T(8,128)(2,1)S(1)}, u32[]{:S(2)}, u32[]{:S(2)}) collective-permute-start(bf16[256,512]{1,0:T(8,128)(2,1)S(1)} %collective-permute-done.6.refs_10_), channel_id=1, source_target_pairs={{0,8},{8,0},{1,9},{9,1},{2,10},{10,2},{3,11},{11,3},{4,12},{12,4},... | collective-permute-start | bytes 786440 | tf_op jit(solution)/shard_map/ppermute | solution.py:157
  44.0 6.4 %collective-permute-start.5 = (bf16[128,512]{1,0:T(8,128)(2,1)S(1)}, bf16[128,512]{1,0:T(8,128)(2,1)S(1)}, u32[]{:S(2)}, u32[]{:S(2)}) collective-permute-start(bf16[128,512]{1,0:T(8,128)(2,1)S(1)} %slice.56), channel_id=1, source_target_pairs={{0,32},{32,64},{64,96},{96,128},{128,160},{160,192},{192,224},{224... | collective-permute-start | bytes 393224 | tf_op jit(solution)/shard_map/ppermute | solution.py:161
  44.1 7.1 %collective-permute-start.9 = (bf16[128,512]{1,0:T(8,128)(2,1)S(1)}, bf16[128,512]{1,0:T(8,128)(2,1)S(1)}, u32[]{:S(2)}, u32[]{:S(2)}) collective-permute-start(bf16[128,512]{1,0:T(8,128)(2,1)S(1)} %slice.57), channel_id=1, source_target_pairs={{0,224},{32,0},{64,32},{96,64},{128,96},{160,128},{192,160},{224,1... | collective-permute-start | bytes 393224 | tf_op jit(solution)/shard_map/ppermute | solution.py:161
  50.4 3.9 %collective-permute-start.12 = (bf16[256,512]{1,0:T(8,128)(2,1)S(1)}, bf16[256,512]{1,0:T(8,128)(2,1)S(1)}, u32[]{:S(2)}, u32[]{:S(2)}) collective-permute-start(bf16[256,512]{1,0:T(8,128)(2,1)S(1)} %collective-permute-done.3.refs_5_), channel_id=1, source_target_pairs={{0,8},{8,0},{1,9},{9,1},{2,10},{10,2},{3,11},{11,3},{4,12},{12,4},... | collective-permute-start | bytes 786440 | tf_op jit(solution)/shard_map/ppermute | solution.py:157
  51.2 3.1 %collective-permute-start.16 = (bf16[256,512]{1,0:T(8,128)(2,1)S(1)}, bf16[256,512]{1,0:T(8,128)(2,1)}, u32[]{:S(2)}, u32[]{:S(2)}) collective-permute-start(bf16[256,512]{1,0:T(8,128)(2,1)S(1)} %collective-permute-done.7.refs_9_), channel_id=1, source_target_pairs={{0,8},{8,0},{1,9},{9,1},{2,10},{10,2},{3,11},{11,3},{4,12},{12,4},... | collective-permute-start | bytes 786440 | tf_op jit(solution)/shard_map/ppermute | solution.py:157
  51.4 3.0 %collective-permute-start.13 = (bf16[256,512]{1,0:T(8,128)(2,1)S(1)}, bf16[256,512]{1,0:T(8,128)(2,1)}, u32[]{:S(2)}, u32[]{:S(2)}) collective-permute-start(bf16[256,512]{1,0:T(8,128)(2,1)S(1)} %collective-permute-done.4.refs_6_), channel_id=1, source_target_pairs={{0,8},{8,0},{1,9},{9,1},{2,10},{10,2},{3,11},{11,3},{4,12},{12,4},... | collective-permute-start | bytes 786440 | tf_op jit(solution)/shard_map/ppermute | solution.py:157
  52.0 2.4 %collective-permute-start.15 = (bf16[256,512]{1,0:T(8,128)(2,1)S(1)}, bf16[256,512]{1,0:T(8,128)(2,1)}, u32[]{:S(2)}, u32[]{:S(2)}) collective-permute-start(bf16[256,512]{1,0:T(8,128)(2,1)S(1)} %collective-permute-done.8.refs_8_), channel_id=1, source_target_pairs={{0,8},{8,0},{1,9},{9,1},{2,10},{10,2},{3,11},{11,3},{4,12},{12,4},... | collective-permute-start | bytes 786440 | tf_op jit(solution)/shard_map/ppermute | solution.py:157
  52.1 2.3 %collective-permute-start.14 = (bf16[256,512]{1,0:T(8,128)(2,1)S(1)}, bf16[256,512]{1,0:T(8,128)(2,1)}, u32[]{:S(2)}, u32[]{:S(2)}) collective-permute-start(bf16[256,512]{1,0:T(8,128)(2,1)S(1)} %constant_dynamic-update-slice_fusion.refs_7_), channel_id=1, source_target_pairs={{0,8},{8,0},{1,9},{9,1},{2,10},{10,2},{3,11},{11,3},{4,12},{12,4},... | collective-permute-start | bytes 786440 | tf_op jit(solution)/shard_map/ppermute | solution.py:157
  60.4 2.7 %collective-permute-start.19 = (bf16[8,256,256]{2,1,0:T(8,128)(2,1)S(1)}, bf16[8,256,256]{2,1,0:T(8,128)(2,1)S(1)}, u32[]{:S(2)}, u32[]{:S(2)}) collective-permute-start(bf16[8,256,256]{2,1,0:T(8,128)(2,1)S(1)} %slice.45), channel_id=1, source_target_pairs={{0,8},{8,0},{1,9},{9,1},{2,10},{10,2},{3,11},{11,3},{4,12},{12,4},... | collective-permute-start | bytes 3145736 | tf_op jit(solution)/shard_map/ppermute | solution.py:157
  65.3 25.4 %copy-start = (bf16[128,4,128]{2,1,0:T(4,128)(2,1)S(1)}, bf16[128,4,128]{2,1,0:T(4,128)(2,1)}, u32[]{:S(2)}) copy-start(bf16[128,4,128]{2,1,0:T(4,128)(2,1)} %param.11) | copy-start | bytes 393220
  66.4 45.4 %copy-start.1 = (bf16[128,2,128]{2,1,0:T(2,128)(2,1)S(1)}, bf16[128,2,128]{2,1,0:T(2,128)(2,1)}, u32[]{:S(2)}) copy-start(bf16[128,2,128]{2,1,0:T(2,128)(2,1)} %param.13) | copy-start | bytes 196612
  66.4 45.4 %copy-start.2 = (bf16[128,2,128]{2,1,0:T(2,128)(2,1)S(1)}, bf16[128,2,128]{2,1,0:T(2,128)(2,1)}, u32[]{:S(2)}) copy-start(bf16[128,2,128]{2,1,0:T(2,128)(2,1)} %param.12) | copy-start | bytes 196612
  66.5 45.6 %copy-start.4 = (s32[128]{0:T(128)S(1)}, s32[128]{0:T(128)}, u32[]{:S(2)}) copy-start(s32[128]{0:T(128)} %param.15) | copy-start | bytes 1540
  66.5 45.2 %all-to-all-start = ((bf16[16,128,256]{2,1,0:T(8,128)(2,1)}), bf16[16,128,256]{2,1,0:T(8,128)(2,1)S(1)}, u32[]{:S(2)}, u32[]{:S(2)}) async-start(bf16[16,128,256]{2,1,0:T(8,128)(2,1)} %broadcast_select_fusion), calls=%async_computation | async-start | bytes 2097152 | tf_op jit(solution)/shard_map/all_to_all | solution.py:225
  86.0 4.5 %collective-permute-start.18 = (bf16[2,128,128]{2,0,1:T(2,128)(2,1)S(1)}, bf16[2,128,128]{2,0,1:T(2,128)(2,1)S(1)}, u32[]{:S(2)}, u32[]{:S(2)}) collective-permute-start(bf16[2,128,128]{2,0,1:T(2,128)(2,1)S(1)} %bitcast.45), channel_id=1, source_target_pairs={{0,16},{16,0},{1,17},{17,1},{2,18},{18,2},{3,19},{19,3},{4,20},{20... | collective-permute-start | bytes 196616 | tf_op jit(solution)/shard_map/ppermute | solution.py:157
  113.0 25.0 %all-to-all-start.1 = ((f32[256,16,1]{1,2,0:T(1,128)}), f32[256,16,1]{1,2,0:T(1,128)S(1)}, u32[]{:S(2)}, u32[]{:S(2)}) async-start(f32[256,16,1]{1,2,0:T(1,128)} %all_to_all.11), calls=%async_computation.1 | async-start | bytes 262144 | tf_op jit(solution)/shard_map/all_to_all | solution.py:241

commit v2 on v1

v2 whole, which is shorter than its diff:
```python
import math

import jax
import jax.numpy as jnp
from jax import lax
from jax.experimental import pallas as pl
from jax.experimental.pallas import tpu as pltpu
from jax.sharding import Mesh, PartitionSpec as P

DOCS = 8
NZ = 8
FAR = NZ // 2
ROWS = 128
HD = 128
DR = 16
PIECE = ROWS + DR
CH = 2 * ROWS
MQ = 2 * CH
BK = 2 * CH
SCALE = 1.0 / 12.0
SCALE2 = SCALE * math.log2(math.e)
LOWEST = -1e30
ALL = ("z", "xl", "c", "h")
BF = jnp.bfloat16
F32 = jnp.float32
VMEM_LIMIT = 28 * 1024 * 1024


def dot(a, b):
    return lax.dot_general(a, b, (((1,), (0,)), ((), ())), preferred_element_type=F32)


def whole_call(kernel, out_shape, *arrays, limit=None):
    vmem = pl.BlockSpec(memory_space=pltpu.VMEM)
    return pl.pallas_call(
        kernel,
        out_shape=out_shape,
        in_specs=[vmem] * len(arrays),
        out_specs=(vmem,) * len(out_shape),
        compiler_params=pltpu.CompilerParams(vmem_limit_bytes=limit),
        cost_estimate=pl.CostEstimate(flops=0, bytes_accessed=1 << 20, transcendentals=0),
    )(*arrays)


def pack_keys_kernel(k, v, kt, vt, docs, kv_mine, kv_other):
    first = lax.axis_index("xl") == 0
    ids = jnp.broadcast_to(docs[...], (DR, HD)).astype(F32).astype(BF)
    for col, ref in enumerate((k, kt, v, vt)):
        a, b = ref[:, 0, :], ref[:, 1, :]
        lanes = pl.ds(col * HD, HD)
        kv_mine[pl.ds(0, ROWS), lanes] = jnp.where(first, a, b)
        kv_other[pl.ds(0, ROWS), lanes] = jnp.where(first, b, a)
        kv_mine[pl.ds(ROWS, DR), lanes] = ids
        kv_other[pl.ds(ROWS, DR), lanes] = ids


def pack_queries_kernel(q, qt, curv, q_mine, q_other):
    first = lax.axis_index("xl") == 0
    for h in range(2):
        for col, ref in enumerate((qt, q)):
            a, b = ref[:, h, :], ref[:, 2 + h, :]
            lanes = pl.ds((2 * h + col) * HD, HD)
            q_mine[pl.ds(0, ROWS), lanes] = jnp.where(first, a, b)
            q_other[pl.ds(0, ROWS), lanes] = jnp.where(first, b, a)
        a, b = curv[pl.ds(h, 1)], curv[pl.ds(2 + h, 1)]
        lanes = pl.ds(2 * h * HD, HD)
        for ref, row in ((q_mine, jnp.where(first, a, b)), (q_other, jnp.where(first, b, a))):
            row = jnp.broadcast_to(row, (DR, HD))
            line = lax.broadcasted_iota(jnp.int32, (DR, HD), 0)
            high = row.astype(BF).astype(F32)
            rest = row - high
            mid = rest.astype(BF).astype(F32)
            parts = jnp.where(line == 0, high, jnp.where(line == 1, mid, rest - mid))
            ref[pl.ds(ROWS, DR), lanes] = jnp.where(line < 3, parts, 0.0).astype(BF)
            ref[pl.ds(ROWS, DR), pl.ds((2 * h + 1) * HD, HD)] = jnp.zeros((DR, HD), BF)


def grads_kernel(parts, key_grad, value_grad):
    for head in range(2):
        total = parts[head].astype(F32)
        for z in range(1, NZ):
            total += parts[2 * z + head].astype(F32)
        key_grad[:, head, :] = total[:, :HD].astype(BF)
        value_grad[:, head, :] = total[:, HD:].astype(BF)


def query_grads_kernel(mine, other, query_grad):
    first = lax.axis_index("xl") == 0
    for h in range(2):
        query_grad[:, h, :] = jnp.where(first, mine[h], other[h])
        query_grad[:, 2 + h, :] = jnp.where(first, other[h], mine[h])


def rows_of(h, s):
    return (h * 2 + s) * ROWS


def masked(scores, xl, core):
    key = lax.broadcasted_iota(jnp.int32, scores.shape, 0)
    row = lax.broadcasted_iota(jnp.int32, scores.shape, 1) % CH
    row_xl = jnp.where(row >= ROWS, 1 - xl, xl)
    row_pos = row_xl * CH + core * ROWS + row % ROWS
    key_core = jnp.where(key >= CH, 1 - core, core)
    key = key % CH
    key_xl = jnp.where(key >= ROWS, 1 - xl, xl)
    key_pos = key_xl * CH + key_core * ROWS + key % ROWS
    return jnp.where(key_pos <= row_pos, scores, LOWEST)


def folded(x, combine):
    return combine(x.reshape(x.shape[0] // 8, 8, x.shape[1]), axis=0)


A0, B0, A1, B1, A2, B2, A3, B3, N4 = range(9)
XA1, XB1, XA2, XB2, XA3, XB3, X4 = range(9, 16)
NS = 16
BLOCKS = ((A0, B0), (A1, B1), (A2, B2), (A3, B3), (N4, X4), (XA3, XB3), (XA2, XB2), (XA1, XB1))


def pieces_of(n):
    out = []
    for side in range(2):
        for at in BLOCKS[n]:
            flip = at >= XA1
            out.append((at, PIECE * (1 - side if flip else side)))
    return out


def attention_kernel(*refs):
    q_refs = refs[:2]
    sources = refs[2 : 2 + NS]
    refs = refs[2 + NS :]
    gq_mine, gq_other, g_own, g_sib, doc_ref, count_ref = refs[:6]
    q_t, q_n, score, acc_v, acc_t, cot_t, cot_n, stat, tops, tots, sprs, doc_acc = refs[6:]
    z = lax.axis_index("z")
    xl = lax.axis_index("xl")
    core = lax.axis_index("c")

    def keys(n, first, last):
        return jnp.concatenate(
            [
                sources[at][row : row + ROWS, first * HD : last * HD]
                for at, row in pieces_of(n)
            ],
            axis=0,
        )

    def onehot(piece):
        at, row = piece
        ids = sources[at][row + ROWS : row + PIECE, :HD].astype(F32).astype(jnp.int32)
        names = lax.broadcasted_iota(jnp.int32, (DR, ROWS), 0)
        return jnp.where(ids == names, 1.0, 0.0)

    def place(n):
        return jnp.where(core == 0, n, NZ - n) if n else 0

    def before(block):
        for n in range(1, NZ):
            pl.when(z >= place(n))(lambda n=n: block(n))

    curv = []
    for h in range(2):
        for s in range(2):
            q = q_refs[s]
            x = q[:ROWS, 2 * h * HD : 2 * (h + 1) * HD]
            q_n[pl.ds(rows_of(h, s), ROWS)] = x
            q_t[:, pl.ds(rows_of(h, s), ROWS)] = x.T
            line = q[ROWS:, 2 * h * HD : (2 * h + 1) * HD].astype(F32)
            curv.append(jnp.sum(line, axis=0, keepdims=True))
    curv = jnp.concatenate(curv, axis=1)

    def scores_of(d, diagonal):
        s = dot(keys(d, 0, 1), q_t[HD:, :])
        if diagonal:
            s = masked(s, xl, core)
        score[d] = s
        top = folded(s, jnp.max)
        tops[...] = top if diagonal else jnp.maximum(tops[...], top)

    scores_of(0, True)
    before(lambda d: scores_of(d, False))
    top = jnp.max(tops[...], axis=0, keepdims=True) * SCALE2
    stat[0:1, :] = top

    def forward(d, diagonal):
        values_t = keys(d, 2, 4).T
        slope = dot(keys(d, 0, 2), q_t[...])
        e = jnp.exp2(score[d] * SCALE2 - stat[0:1, :])
        f = e * slope
        part_v = dot(values_t, e.astype(BF))
        part_t = dot(values_t[:HD], f.astype(BF))
        tot, spr = folded(e, jnp.sum), folded(f, jnp.sum)
        if diagonal:
            acc_v[...], acc_t[...], tots[...], sprs[...] = part_v, part_t, tot, spr
        else:
            acc_v[...] += part_v
            acc_t[...] += part_t
            tots[...] += tot
            sprs[...] += spr

    forward(0, True)
    before(lambda d: forward(d, False))

    tot = jnp.sum(tots[...], axis=0, keepdims=True)
    spr = jnp.sum(sprs[...], axis=0, keepdims=True) * SCALE
    inv = 1.0 / tot
    out = acc_v[:HD, :] * inv
    out_tan = (acc_t[...] * SCALE + acc_v[HD:, :]) * inv - (spr * inv) * out
    cot = (curv * out_tan).astype(BF)
    cot_t[...] = cot
    cot_n[...] = cot.T
    stat[1:2, :] = stat[0:1, :] + jnp.log2(tot)
    stat[2:3, :] = jnp.sum(cot.astype(F32) * out, axis=0, keepdims=True)
    acc_t[...] = jnp.zeros((HD, MQ), F32)
    doc_acc[...] = jnp.zeros((DR, HD), F32)

    def by_document(hots, terms):
        hot = jnp.concatenate(hots, axis=1).astype(BF)
        high = terms.astype(BF)
        low = (terms - high.astype(F32)).astype(BF)
        return dot(hot, high) + dot(hot, low)

    def backward(d):
        keys_t = keys(d, 0, 1).T
        p = jnp.exp2(score[d] * SCALE2 - stat[1:2, :])
        push = dot(keys(d, 2, 3), cot_t[...])
        g = (p * (push - stat[2:3, :])).astype(BF)
        acc_t[...] += dot(keys_t, g)
        gk = dot(g, q_n[:, HD:]) * SCALE
        gv = dot(p.astype(BF), cot_n[...])
        terms = gk * keys(d, 1, 2).astype(F32) + gv * keys(d, 3, 4).astype(F32)
        for side, g_ref in enumerate((g_own, g_sib)):
            for s in range(2):
                at = side * CH + s * ROWS
                to_xl = xl if s == 0 else 1 - xl
                if d == FAR:
                    to_xl = jnp.where(core == 0, to_xl, 1 - to_xl)
                g_ref[z - place(d), to_xl, :, :HD] = gk[at : at + ROWS].astype(BF)
                g_ref[z - place(d), to_xl, :, HD:] = gv[at : at + ROWS].astype(BF)
        doc_acc[...] += by_document([onehot(p) for p in pieces_of(d)], terms)

    backward(0)
    before(backward)

    @pl.loop(z + 1, NZ)
    def _(to):
        g_own[to] = jnp.zeros((2, ROWS, 2 * HD), BF)
        g_sib[to] = jnp.zeros((2, ROWS, 2 * HD), BF)

    counts = sum(onehot(p) for n in range(NZ) for p in pieces_of(n))
    count_ref[...] = jnp.broadcast_to(jnp.sum(counts, axis=1, keepdims=True), (DR, ROWS))
    gq = (acc_t[...] * SCALE).T
    terms = gq * q_n[:, :HD].astype(F32)
    hots = [onehot(p) for p in pieces_of(0)[:2]]
    doc = doc_acc[...] + by_document(hots * 2, terms)
    for h in range(2):
        for s, ref in enumerate((gq_mine, gq_other)):
            ref[h] = gq[rows_of(h, s) : rows_of(h, s) + ROWS].astype(BF)
    doc_ref[...] = jnp.broadcast_to(jnp.sum(doc, axis=1, keepdims=True), (DR, HD))


def attention(q, sources):
    vmem = pl.BlockSpec(memory_space=pltpu.VMEM)
    gq_shape = jax.ShapeDtypeStruct((2, ROWS, HD), BF)
    g_shape = jax.ShapeDtypeStruct((NZ, 2, ROWS, 2 * HD), BF)
    line_shape = jax.ShapeDtypeStruct((DR, HD), F32)
    return pl.pallas_call(
        attention_kernel,
        out_shape=(gq_shape, gq_shape, g_shape, g_shape, line_shape, line_shape),
        in_specs=[vmem] * (2 + len(sources)),
        out_specs=(vmem,) * 6,
        scratch_shapes=[
            pltpu.VMEM((2 * HD, MQ), BF),
            pltpu.VMEM((MQ, 2 * HD), BF),
            pltpu.VMEM((NZ, BK, MQ), F32),
            pltpu.VMEM((2 * HD, MQ), F32),
            pltpu.VMEM((HD, MQ), F32),
            pltpu.VMEM((HD, MQ), BF),
            pltpu.VMEM((MQ, HD), BF),
            pltpu.VMEM((8, MQ), F32),
            pltpu.VMEM((8, MQ), F32),
            pltpu.VMEM((8, MQ), F32),
            pltpu.VMEM((8, MQ), F32),
            pltpu.VMEM((DR, HD), F32),
        ],
        compiler_params=pltpu.CompilerParams(vmem_limit_bytes=VMEM_LIMIT),
        cost_estimate=pl.CostEstimate(
            flops=8 * 2 * MQ * 4096 * 256, bytes_accessed=8 << 20, transcendentals=2 * MQ * 4096
        ),
    )(*q, *sources)


def swap(x, axis):
    return lax.ppermute(x, axis, [(0, 1), (1, 0)])


def around(x):
    pairs = [(2 * i + c, 2 * ((i + step) % NZ) + c) for i in range(NZ) for c, step in ((0, 1), (1, -1))]
    return lax.ppermute(x, ("z", "c"), pairs)


def bundle(x):
    return jnp.concatenate([x, swap(x, "c")], axis=0)


def sum_of_four(x, axes, size, one, two):
    got = [
        lax.ppermute(x, axes, [(i, i ^ m) for i in range(size)]) for m in (one, two, one ^ two)
    ]
    return (x + got[0]) + (got[1] + got[2])


def on_device(
    query_rows,
    key_rows,
    value_rows,
    query_tangent,
    key_tangent,
    value_tangent,
    curvature,
    documents,
):
    piece = jax.ShapeDtypeStruct((PIECE, 4 * HD), BF)
    kv_mine, kv_other = whole_call(
        pack_keys_kernel, (piece, piece),
        key_rows, value_rows, key_tangent, value_tangent, documents.reshape(1, ROWS),
    )
    kv_other = swap(kv_other, "xl")
    a = [bundle(kv_mine)]
    a[0], query_rows = lax.optimization_barrier((a[0], query_rows))
    a.append(around(a[0]))
    q_mine, q_other = whole_call(
        pack_queries_kernel, (piece, piece), query_rows, query_tangent, curvature
    )
    kv_other, q_other = lax.optimization_barrier((kv_other, q_other))
    b = [bundle(kv_other)]
    b.append(around(b[0]))
    crossed = []
    for k in range(1, FAR):
        late_a, b[k], q_other = lax.optimization_barrier((a[k], b[k], q_other))
        if k == 1:
            q_other = swap(q_other, "xl")
        crossed.append(swap(late_a, "c"))
        if k < FAR - 1:
            a.append(around(a[k]))
            late_b, _ = lax.optimization_barrier((b[k], a[k + 1]))
            crossed.append(swap(late_b, "c"))
            b.append(around(b[k]))
    crossed.append(swap(b[FAR - 1], "c"))
    far = around(jnp.where(lax.axis_index("c") == 0, a[FAR - 1], b[FAR - 1]))
    native = [x for pair in zip(a, b) for x in pair]
    gq_mine, gq_other, g_own, g_sib, doc, count = attention(
        (q_mine, q_other), native + [far] + crossed + [swap(far, "c")]
    )

    from_sibling = swap(g_sib, "c")
    doc = sum_of_four(doc, ("z", "xl", "c"), 32, 4, 1)
    part = (g_own.astype(F32) + from_sibling.astype(F32)).astype(BF)
    part, doc = lax.optimization_barrier((part, doc))
    part = lax.all_to_all(part.reshape(2 * NZ, ROWS, 2 * HD), ("z", "xl"), 0, 0, tiled=True)
    grad_shape = jax.ShapeDtypeStruct((ROWS, 2, HD), BF)
    key_grad, value_grad = whole_call(
        grads_kernel, (grad_shape, grad_shape), part, limit=VMEM_LIMIT
    )

    gq_other = swap(gq_other, "xl")
    (query_grad,) = whole_call(
        query_grads_kernel, (jax.ShapeDtypeStruct((ROWS, 4, HD), BF),), gq_mine, gq_other,
        limit=VMEM_LIMIT,
    )

    doc = sum_of_four(doc, "h", 8, 2, 4)
    doc = sum_of_four(doc, ("xl", "h"), 16, 8, 1)
    doc = sum_of_four(doc, "z", 8, 2, 4)
    doc, key_grad = lax.optimization_barrier((doc, key_grad))
    doc_scores = doc[:DOCS, 0] / (count[:DOCS, 0] * (32 * HD))
    return (query_grad, key_grad, value_grad, doc_scores)


def solution(mesh):
    split = Mesh(mesh.devices.reshape(NZ, 2, 2, 8), ALL)
    ctx = ("z", "xl", "c")
    rows = P(ctx, "h", None)
    in_specs = (rows,) * 6 + (P("h", ctx), P(ctx))
    out_specs = (rows, rows, rows, P())
    return jax.shard_map(
        on_device, mesh=split, in_specs=in_specs, out_specs=out_specs, check_vma=False
    )
```

time: 140 us -> 103 us (0.74)
  the two profiles are of different devices: /device:TPU:1 before, /device:TPU:8 now
where the time goes in v2:
time: 103 us
  waiting for transfers between devices  45.4 us (44%)
  starting transfers between devices  43.4 us (42%)
  Pallas kernels  10.2 us (10%)
  other arithmetic  2.93 us (3%)
    ppermute x7, waiting for transfers between devices, around(): return lax.ppermute(x, ('z', 'c'), pairs)  29 us
    ppermute x12, starting transfers between devices, sum_of_four(): lax.ppermute(x, axes, [(i, i ^ m) for i in range(size)])  17.1 us
    all_to_all x1, starting transfers between devices, on_device(): lax.all_to_all(part.reshape(2 * NZ, ROWS, 2 * HD), ('z', 'xl'), 0, 0, til...  14.9 us
    ppermute x12, waiting for transfers between devices, sum_of_four(): lax.ppermute(x, axes, [(i, i ^ m) for i in range(size)])  12.6 us
    pallas_call x4, Pallas kernels, whole_call(): pl.pallas_call(kernel, out_shape=out_shape, in_specs=[vmem] * len(arrays)...  7.73 us
    ppermute x13, starting transfers between devices, swap(): return lax.ppermute(x, axis, [(0, 1), (1, 0)])  7.47 us
    ppermute x7, starting transfers between devices, around(): return lax.ppermute(x, ('z', 'c'), pairs)  4.01 us
    ppermute x13, waiting for transfers between devices, swap(): return lax.ppermute(x, axis, [(0, 1), (1, 0)])  3.81 us
  transfers between devices with their start and end apart: 33, of which 17 were waited for; matrix products, arithmetic and copies ran while one was open for 1% of the time, Pallas kernels for 4%

profile of v2, /device:TPU:8, one launch (start us, length us, event | category | flops | bytes accessed | tf_op | source)
XLA Modules:
  0.0 102.7 jit_solution(2028254160453058530)
XLA Ops:
  0.6 2.7 %shard_map.111 = (bf16[144,512]{1,0:T(8,128)(2,1)}, bf16[144,512]{1,0:T(8,128)(2,1)}) custom-call(bf16[128,2,128]{2,1,0:T(2,128)(2,1)} %k.1, bf16[128,2,128]{2,1,0:T(2,128)(2,1)} %v.1, bf16[128,2,128]{2,1,0:T(2,128)(2,1)} %kt.1, bf16[128,2,128]{2,1,0:T(2,128)(2,1)} %vt.1, s32[1,128]{1,0:T(1,128)} %bitcast.2), custom_call_target="tpu_custom_call" | custom-call | bytes 1048576 | tf_op jit(solution)/shard_map/pallas_call | solution.py:35
  3.4 1.5 %collective-permute-start.4 = (bf16[144,512]{1,0:T(8,128)(2,1)}, bf16[144,512]{1,0:T(8,128)(2,1)S(1)}, u32[]{:S(2)}, u32[]{:S(2)}) collective-permute-start(bf16[144,512]{1,0:T(8,128)(2,1)} %get-tuple-element.39), channel_id=1, source_target_pairs={{0,16},{16,0},{1,17},{17,1},{2,18},{18,2},{3,19},{19,3},{4,20},{20... | collective-permute-start | bytes 442376 | tf_op jit(solution)/shard_map/ppermute | solution.py:294
  5.9 2.6 %shard_map.112 = (bf16[144,512]{1,0:T(8,128)(2,1)}, bf16[144,512]{1,0:T(8,128)(2,1)}) custom-call(bf16[128,4,128]{2,1,0:T(4,128)(2,1)} %q, bf16[128,4,128]{2,1,0:T(4,128)(2,1)} %qt.1, f32[4,128]{1,0:T(4,128)} %curv.1), custom_call_target="tpu_custom_call" | custom-call | bytes 1048576 | tf_op jit(solution)/shard_map/pallas_call | solution.py:35
  8.5 1.4 %collective-permute-done.4 = bf16[144,512]{1,0:T(8,128)(2,1)S(1)} collective-permute-done((bf16[144,512]{1,0:T(8,128)(2,1)}, bf16[144,512]{1,0:T(8,128)(2,1)S(1)}, u32[]{:S(2)}, u32[]{:S(2)}) %collective-permute-start.4) | collective-permute-done | bytes 147488 | tf_op jit(solution)/shard_map/ppermute | solution.py:294
  9.8 1.9 %collective-permute-start.1 = (bf16[288,512]{1,0:T(8,128)(2,1)S(1)}, bf16[288,512]{1,0:T(8,128)(2,1)S(1)}, u32[]{:S(2)}, u32[]{:S(2)}) collective-permute-start(bf16[288,512]{1,0:T(8,128)(2,1)S(1)} %pad_maximum_fusion.refs_2_), channel_id=1, source_target_pairs={{0,32},{8,232},{32,64},{40,8},{64,96},{72,40},{96,128},{104,72},{1... | collective-permute-start | bytes 884744 | tf_op jit(solution)/shard_map/ppermute | solution.py:299
  11.8 2.0 %collective-permute-start.6 = (bf16[288,512]{1,0:T(8,128)(2,1)S(1)}, bf16[288,512]{1,0:T(8,128)(2,1)S(1)}, u32[]{:S(2)}, u32[]{:S(2)}) collective-permute-start(bf16[288,512]{1,0:T(8,128)(2,1)S(1)} %constant_dynamic-update-slice_fusion.refs_3_), channel_id=1, source_target_pairs={{0,32},{8,232},{32,64},{40,8},{64,96},{72,40},{96,128},{104,72},{1... | collective-permute-start | bytes 884744 | tf_op jit(solution)/shard_map/ppermute | solution.py:299
  13.8 6.6 %collective-permute-done.1.refs_4_ = bf16[288,512]{1,0:T(8,128)(2,1)S(1)} collective-permute-done((bf16[288,512]{1,0:T(8,128)(2,1)S(1)}, bf16[288,512]{1,0:T(8,128)(2,1)S(1)}, u32[]{:S(2)}, u32[]{:S(2)}) %collective-permute-start.1) | collective-permute-done | bytes 294944 | tf_op jit(solution)/shard_map/ppermute | solution.py:299
  20.4 3.2 %collective-permute-done.6.refs_5_ = bf16[288,512]{1,0:T(8,128)(2,1)S(1)} collective-permute-done((bf16[288,512]{1,0:T(8,128)(2,1)S(1)}, bf16[288,512]{1,0:T(8,128)(2,1)S(1)}, u32[]{:S(2)}, u32[]{:S(2)}) %collective-permute-start.6) | collective-permute-done | bytes 294944 | tf_op jit(solution)/shard_map/ppermute | solution.py:299
  23.6 1.5 %collective-permute-start.8 = (bf16[144,512]{1,0:T(8,128)(2,1)}, bf16[144,512]{1,0:T(8,128)(2,1)S(1)}, u32[]{:S(2)}, u32[]{:S(2)}) collective-permute-start(bf16[144,512]{1,0:T(8,128)(2,1)} %get-tuple-element.44), channel_id=1, source_target_pairs={{0,16},{16,0},{1,17},{17,1},{2,18},{18,2},{3,19},{19,3},{4,20},{20... | collective-permute-start | bytes 442376 | tf_op jit(solution)/shard_map/ppermute | solution.py:294
  25.1 3.3 %collective-permute-done.2.refs_6_ = bf16[288,512]{1,0:T(8,128)(2,1)S(1)} collective-permute-done((bf16[288,512]{1,0:T(8,128)(2,1)S(1)}, bf16[288,512]{1,0:T(8,128)(2,1)S(1)}, u32[]{:S(2)}, u32[]{:S(2)}) %collective-permute-start.2) | collective-permute-done | bytes 294944 | tf_op jit(solution)/shard_map/ppermute | solution.py:299
  29.1 2.4 %collective-permute-done.7.refs_7_ = bf16[288,512]{1,0:T(8,128)(2,1)S(1)} collective-permute-done((bf16[288,512]{1,0:T(8,128)(2,1)S(1)}, bf16[288,512]{1,0:T(8,128)(2,1)S(1)}, u32[]{:S(2)}, u32[]{:S(2)}) %collective-permute-start.7) | collective-permute-done | bytes 294944 | tf_op jit(solution)/shard_map/ppermute | solution.py:299
  32.7 3.6 %collective-permute-done.3.refs_8_ = bf16[288,512]{1,0:T(8,128)(2,1)S(1)} collective-permute-done((bf16[288,512]{1,0:T(8,128)(2,1)S(1)}, bf16[288,512]{1,0:T(8,128)(2,1)S(1)}, u32[]{:S(2)}, u32[]{:S(2)}) %collective-permute-start.3) | collective-permute-done | bytes 294944 | tf_op jit(solution)/shard_map/ppermute | solution.py:299
  36.3 3.2 %collective-permute-done.9.refs_9_ = bf16[288,512]{1,0:T(8,128)(2,1)S(1)} collective-permute-done((bf16[288,512]{1,0:T(8,128)(2,1)S(1)}, bf16[288,512]{1,0:T(8,128)(2,1)S(1)}, u32[]{:S(2)}, u32[]{:S(2)}) %collective-permute-start.9) | collective-permute-done | bytes 294944 | tf_op jit(solution)/shard_map/ppermute | solution.py:299
  40.7 6.8 %collective-permute-done.10.refs_10_ = bf16[288,512]{1,0:T(8,128)(2,1)S(1)} collective-permute-done((bf16[288,512]{1,0:T(8,128)(2,1)S(1)}, bf16[288,512]{1,0:T(8,128)(2,1)S(1)}, u32[]{:S(2)}, u32[]{:S(2)}) %collective-permute-start.10) | collective-permute-done | bytes 294944 | tf_op jit(solution)/shard_map/ppermute | solution.py:299
  47.5 1.5 %collective-permute-done.17.refs_17_ = bf16[288,512]{1,0:T(8,128)(2,1)S(1)} collective-permute-done((bf16[288,512]{1,0:T(8,128)(2,1)S(1)}, bf16[288,512]{1,0:T(8,128)(2,1)S(1)}, u32[]{:S(2)}, u32[]{:S(2)}) %collective-permute-start.17) | collective-permute-done | bytes 294944 | tf_op jit(solution)/shard_map/ppermute | solution.py:294
  49.1 2.4 %shard_map.113 = (bf16[2,128,128]{2,1,0:T(8,128)(2,1)S(1)}, bf16[2,128,128]{2,1,0:T(8,128)(2,1)S(1)}, bf16[8,2,128,256]{3,2,1,0:T(8,128)(2,1)S(1)}, bf16[8,2,128...) custom-call(bf16[144,512]{1,0:T(8,128)(2,1)S(1)} %copy-done, ...), custom_call_target="tpu_custom_call" | custom-call | flops 8589934592 | bytes 8388608 | tf_op jit(solution)/shard_map/pallas_call | solution.py:267
  52.5 1.5 %collective-permute-start.20 = (f32[16,128]{1,0:T(8,128)S(1)}, f32[16,128]{1,0:T(8,128)S(1)}, u32[]{:S(2)}, u32[]{:S(2)}) collective-permute-start(f32[16,128]{1,0:T(8,128)S(1)} %get-tuple-element.58), channel_id=1, source_target_pairs={{0,32},{8,40},{16,48},{24,56},{32,0},{40,8},{48,16},{56,24},{64,96... | collective-permute-start | bytes 24584 | tf_op jit(solution)/shard_map/ppermute | solution.py:308
  55.0 1.2 %collective-permute-done.20 = f32[16,128]{1,0:T(8,128)S(1)} collective-permute-done((f32[16,128]{1,0:T(8,128)S(1)}, f32[16,128]{1,0:T(8,128)S(1)}, u32[]{:S(2)}, u32[]{:S(2)}) %collective-permute-start.20) | collective-permute-done | bytes 8224 | tf_op jit(solution)/shard_map/ppermute | solution.py:308
  56.2 1.3 %add_convert_fusion = bf16[8,2,128,256]{3,2,1,0:T(8,128)(2,1)} fusion(bf16[8,2,128,256]{3,2,1,0:T(8,128)(2,1)S(1)} %collective-permute-done.19, bf16[8,2,128,256]{3,2,1,0:T(8,128)(2,1)S(1)} %get-tuple-element.56), kind=kLoop, calls=%fused_computation | loop fusion | flops 2097152 | bytes 3145728 | tf_op jit(solution)/shard_map/convert_element_type | solution.py:358
  57.5 14.9 %all-to-all-start = ((bf16[16,128,256]{2,1,0:T(8,128)(2,1)}), bf16[16,128,256]{2,1,0:T(8,128)(2,1)S(1)}, u32[]{:S(2)}, u32[]{:S(2)}) async-start(bf16[16,128,256]{2,1,0:T(8,128)(2,1)} %bitcast.1), calls=%async_computation | async-start | bytes 2097152 | tf_op jit(solution)/shard_map/all_to_all | solution.py:360
  72.3 1.7 %collective-permute-start.25 = (f32[16,128]{1,0:T(8,128)S(1)}, f32[16,128]{1,0:T(8,128)S(1)}, u32[]{:S(2)}, u32[]{:S(2)}) collective-permute-start(f32[16,128]{1,0:T(8,128)S(1)} %add_add_fusion.3), channel_id=1, source_target_pairs={{0,6},{1,7},{2,4},{3,5},{4,2},{5,3},{6,0},{7,1},{8,14},{9,15},{10,... | collective-permute-start | bytes 24584 | tf_op jit(solution)/shard_map/ppermute | solution.py:308
  74.9 1.6 %collective-permute-start.23 = (f32[16,128]{1,0:T(8,128)S(1)}, f32[16,128]{1,0:T(8,128)S(1)}, u32[]{:S(2)}, u32[]{:S(2)}) collective-permute-start(f32[16,128]{1,0:T(8,128)S(1)} %add_add_fusion.3), channel_id=1, source_target_pairs={{0,2},{1,3},{2,0},{3,1},{4,6},{5,7},{6,4},{7,5},{8,10},{9,11},{10,... | collective-permute-start | bytes 24584 | tf_op jit(solution)/shard_map/ppermute | solution.py:308
  76.5 2.7 %collective-permute-done.24 = f32[16,128]{1,0:T(8,128)S(1)} collective-permute-done((f32[16,128]{1,0:T(8,128)S(1)}, f32[16,128]{1,0:T(8,128)S(1)}, u32[]{:S(2)}, u32[]{:S(2)}) %collective-permute-start.24) | collective-permute-done | bytes 8224 | tf_op jit(solution)/shard_map/ppermute | solution.py:308
  79.2 3.2 %collective-permute-start.28 = (f32[16,128]{1,0:T(8,128)S(1)}, f32[16,128]{1,0:T(8,128)S(1)}, u32[]{:S(2)}, u32[]{:S(2)}) collective-permute-start(f32[16,128]{1,0:T(8,128)S(1)} %add_add_fusion.2), channel_id=1, source_target_pairs={{0,17},{1,16},{2,19},{3,18},{4,21},{5,20},{6,23},{7,22},{16,1},{17... | collective-permute-start | bytes 24584 | tf_op jit(solution)/shard_map/ppermute | solution.py:308
  83.4 1.8 %collective-permute-start.18 = (bf16[2,128,128]{2,1,0:T(8,128)(2,1)S(1)}, bf16[2,128,128]{2,1,0:T(8,128)(2,1)S(1)}, u32[]{:S(2)}, u32[]{:S(2)}) collective-permute-start(bf16[2,128,128]{2,1,0:T(8,128)(2,1)S(1)} %get-tuple-element.55), channel_id=1, source_target_pairs={{0,16},{16,0},{1,17},{17,1},{2,18},{18,2},{3,19},{19,3},{4,20},{20... | collective-permute-start | bytes 196616 | tf_op jit(solution)/shard_map/ppermute | solution.py:294
  85.2 2.4 %collective-permute-done.27 = f32[16,128]{1,0:T(8,128)S(1)} collective-permute-done((f32[16,128]{1,0:T(8,128)S(1)}, f32[16,128]{1,0:T(8,128)S(1)}, u32[]{:S(2)}, u32[]{:S(2)}) %collective-permute-start.27) | collective-permute-done | bytes 8224 | tf_op jit(solution)/shard_map/ppermute | solution.py:308
  87.6 3.7 %collective-permute-start.31 = (f32[16,128]{1,0:T(8,128)S(1)}, f32[16,128]{1,0:T(8,128)S(1)}, u32[]{:S(2)}, u32[]{:S(2)}) collective-permute-start(f32[16,128]{1,0:T(8,128)S(1)} %add_add_fusion.1), channel_id=1, source_target_pairs={{0,192},{32,224},{64,128},{96,160},{128,64},{160,96},{192,0},{224,... | collective-permute-start | bytes 24584 | tf_op jit(solution)/shard_map/ppermute | solution.py:308
  91.3 2.4 %collective-permute-start.30 = (f32[16,128]{1,0:T(8,128)S(1)}, f32[16,128]{1,0:T(8,128)S(1)}, u32[]{:S(2)}, u32[]{:S(2)}) collective-permute-start(f32[16,128]{1,0:T(8,128)S(1)} %add_add_fusion.1), channel_id=1, source_target_pairs={{0,128},{32,160},{64,192},{96,224},{128,0},{160,32},{192,64},{224,... | collective-permute-start | bytes 24584 | tf_op jit(solution)/shard_map/ppermute | solution.py:308
  94.2 1.2 %shard_map.114 = bf16[128,4,128]{2,1,0:T(4,128)(2,1)} custom-call(bf16[2,128,128]{2,1,0:T(8,128)(2,1)S(1)} %get-tuple-element.54.mine, bf16[2,128,128]{2,1,0:T(8,128)(2,1)S(1)} %collective-permute-done.18.other), custom_call_target="tpu_custom_call" | custom-call | bytes 1048576 | tf_op jit(solution)/shard_map/pallas_call | solution.py:35
  95.4 3.4 %collective-permute-done.31 = f32[16,128]{1,0:T(8,128)S(1)} collective-permute-done((f32[16,128]{1,0:T(8,128)S(1)}, f32[16,128]{1,0:T(8,128)S(1)}, u32[]{:S(2)}, u32[]{:S(2)}) %collective-permute-start.31) | collective-permute-done | bytes 8224 | tf_op jit(solution)/shard_map/ppermute | solution.py:308
  98.8 2.1 %collective-permute-done.30 = f32[16,128]{1,0:T(8,128)S(1)} collective-permute-done((f32[16,128]{1,0:T(8,128)S(1)}, f32[16,128]{1,0:T(8,128)S(1)}, u32[]{:S(2)}, u32[]{:S(2)}) %collective-permute-start.30) | collective-permute-done | bytes 8224 | tf_op jit(solution)/shard_map/ppermute | solution.py:308
  100.9 1.2 %shard_map.115 = (bf16[128,2,128]{2,1,0:T(2,128)(2,1)}, bf16[128,2,128]{2,1,0:T(2,128)(2,1)}) custom-call(bf16[16,128,256]{2,1,0:T(8,128)(2,1)S(1)} %all-to-all-done.parts), custom_call_target="tpu_custom_call" | custom-call | bytes 1048576 | tf_op jit(solution)/shard_map/pallas_call | solution.py:35
  (51 shorter events, 9.3 us)
Async XLA Ops:
  3.4 6.5 %collective-permute-start.4 = (bf16[144,512]{1,0:T(8,128)(2,1)}, bf16[144,512]{1,0:T(8,128)(2,1)S(1)}, u32[]{:S(2)}, u32[]{:S(2)}) collective-permute-start(bf16[144,512]{1,0:T(8,128)(2,1)} %get-tuple-element.39), channel_id=1, source_target_pairs={{0,16},{16,0},{1,17},{17,1},{2,18},{18,2},{3,19},{19,3},{4,20},{20... | collective-permute-start | bytes 442376 | tf_op jit(solution)/shard_map/ppermute | solution.py:294
  9.8 1.9 %collective-permute-start.5 = (bf16[144,512]{1,0:T(8,128)(2,1)S(1)}, bf16[144,512]{1,0:T(8,128)(2,1)S(1)}, u32[]{:S(2)}, u32[]{:S(2)}) collective-permute-start(bf16[144,512]{1,0:T(8,128)(2,1)S(1)} %collective-permute-done.4), channel_id=1, source_target_pairs={{0,8},{8,0},{1,9},{9,1},{2,10},{10,2},{3,11},{11,3},{4,12},{12,4},... | collective-permute-start | bytes 442376 | tf_op jit(solution)/shard_map/ppermute | solution.py:294
  9.8 10.6 %collective-permute-start.1 = (bf16[288,512]{1,0:T(8,128)(2,1)S(1)}, bf16[288,512]{1,0:T(8,128)(2,1)S(1)}, u32[]{:S(2)}, u32[]{:S(2)}) collective-permute-start(bf16[288,512]{1,0:T(8,128)(2,1)S(1)} %pad_maximum_fusion.refs_2_), channel_id=1, source_target_pairs={{0,32},{8,232},{32,64},{40,8},{64,96},{72,40},{96,128},{104,72},{1... | collective-permute-start | bytes 884744 | tf_op jit(solution)/shard_map/ppermute | solution.py:299
  11.8 11.8 %collective-permute-start.6 = (bf16[288,512]{1,0:T(8,128)(2,1)S(1)}, bf16[288,512]{1,0:T(8,128)(2,1)S(1)}, u32[]{:S(2)}, u32[]{:S(2)}) collective-permute-start(bf16[288,512]{1,0:T(8,128)(2,1)S(1)} %constant_dynamic-update-slice_fusion.refs_3_), channel_id=1, source_target_pairs={{0,32},{8,232},{32,64},{40,8},{64,96},{72,40},{96,128},{104,72},{1... | collective-permute-start | bytes 884744 | tf_op jit(solution)/shard_map/ppermute | solution.py:299
  20.4 7.9 %collective-permute-start.2 = (bf16[288,512]{1,0:T(8,128)(2,1)S(1)}, bf16[288,512]{1,0:T(8,128)(2,1)S(1)}, u32[]{:S(2)}, u32[]{:S(2)}) collective-permute-start(bf16[288,512]{1,0:T(8,128)(2,1)S(1)} %collective-permute-done.1.refs_4_), channel_id=1, source_target_pairs={{0,32},{8,232},{32,64},{40,8},{64,96},{72,40},{96,128},{104,72},{1... | collective-permute-start | bytes 884744 | tf_op jit(solution)/shard_map/ppermute | solution.py:299
  23.6 7.9 %collective-permute-start.7 = (bf16[288,512]{1,0:T(8,128)(2,1)S(1)}, bf16[288,512]{1,0:T(8,128)(2,1)S(1)}, u32[]{:S(2)}, u32[]{:S(2)}) collective-permute-start(bf16[288,512]{1,0:T(8,128)(2,1)S(1)} %collective-permute-done.6.refs_5_), channel_id=1, source_target_pairs={{0,32},{8,232},{32,64},{40,8},{64,96},{72,40},{96,128},{104,72},{1... | collective-permute-start | bytes 884744 | tf_op jit(solution)/shard_map/ppermute | solution.py:299
  23.6 5.6 %collective-permute-start.8 = (bf16[144,512]{1,0:T(8,128)(2,1)}, bf16[144,512]{1,0:T(8,128)(2,1)S(1)}, u32[]{:S(2)}, u32[]{:S(2)}) collective-permute-start(bf16[144,512]{1,0:T(8,128)(2,1)} %get-tuple-element.44), channel_id=1, source_target_pairs={{0,16},{16,0},{1,17},{17,1},{2,18},{18,2},{3,19},{19,3},{4,20},{20... | collective-permute-start | bytes 442376 | tf_op jit(solution)/shard_map/ppermute | solution.py:294
  28.3 7.9 %collective-permute-start.3 = (bf16[288,512]{1,0:T(8,128)(2,1)S(1)}, bf16[288,512]{1,0:T(8,128)(2,1)S(1)}, u32[]{:S(2)}, u32[]{:S(2)}) collective-permute-start(bf16[288,512]{1,0:T(8,128)(2,1)S(1)} %collective-permute-done.2.refs_6_), channel_id=1, source_target_pairs={{0,32},{8,232},{32,64},{40,8},{64,96},{72,40},{96,128},{104,72},{1... | collective-permute-start | bytes 884744 | tf_op jit(solution)/shard_map/ppermute | solution.py:299
  31.5 7.9 %collective-permute-start.9 = (bf16[288,512]{1,0:T(8,128)(2,1)S(1)}, bf16[288,512]{1,0:T(8,128)(2,1)S(1)}, u32[]{:S(2)}, u32[]{:S(2)}) collective-permute-start(bf16[288,512]{1,0:T(8,128)(2,1)S(1)} %collective-permute-done.7.refs_7_), channel_id=1, source_target_pairs={{0,32},{8,232},{32,64},{40,8},{64,96},{72,40},{96,128},{104,72},{1... | collective-permute-start | bytes 884744 | tf_op jit(solution)/shard_map/ppermute | solution.py:299
  31.5 8.7 %collective-permute-start.11 = (bf16[288,512]{1,0:T(8,128)(2,1)S(1)}, bf16[288,512]{1,0:T(8,128)(2,1)S(1)}, u32[]{:S(2)}, u32[]{:S(2)}) collective-permute-start(bf16[288,512]{1,0:T(8,128)(2,1)S(1)} %collective-permute-done.1.refs_4_), channel_id=1, source_target_pairs={{0,8},{8,0},{1,9},{9,1},{2,10},{10,2},{3,11},{11,3},{4,12},{12,4},... | collective-permute-start | bytes 884744 | tf_op jit(solution)/shard_map/ppermute | solution.py:294
  32.7 7.6 %collective-permute-start.12 = (bf16[288,512]{1,0:T(8,128)(2,1)S(1)}, bf16[288,512]{1,0:T(8,128)(2,1)S(1)}, u32[]{:S(2)}, u32[]{:S(2)}) collective-permute-start(bf16[288,512]{1,0:T(8,128)(2,1)S(1)} %collective-permute-done.6.refs_5_), channel_id=1, source_target_pairs={{0,8},{8,0},{1,9},{9,1},{2,10},{10,2},{3,11},{11,3},{4,12},{12,4},... | collective-permute-start | bytes 884744 | tf_op jit(solution)/shard_map/ppermute | solution.py:294
  39.5 8.0 %collective-permute-start.10 = (bf16[288,512]{1,0:T(8,128)(2,1)S(1)}, bf16[288,512]{1,0:T(8,128)(2,1)S(1)}, u32[]{:S(2)}, u32[]{:S(2)}) collective-permute-start(bf16[288,512]{1,0:T(8,128)(2,1)S(1)} %broadcast_select_fusion), channel_id=1, source_target_pairs={{0,32},{8,232},{32,64},{40,8},{64,96},{72,40},{96,128},{104,72},{1... | collective-permute-start | bytes 884744 | tf_op jit(solution)/shard_map/ppermute | solution.py:299
  39.6 7.9 %collective-permute-start.13 = (bf16[288,512]{1,0:T(8,128)(2,1)S(1)}, bf16[288,512]{1,0:T(8,128)(2,1)S(1)}, u32[]{:S(2)}, u32[]{:S(2)}) collective-permute-start(bf16[288,512]{1,0:T(8,128)(2,1)S(1)} %collective-permute-done.2.refs_6_), channel_id=1, source_target_pairs={{0,8},{8,0},{1,9},{9,1},{2,10},{10,2},{3,11},{11,3},{4,12},{12,4},... | collective-permute-start | bytes 884744 | tf_op jit(solution)/shard_map/ppermute | solution.py:294
  39.7 7.8 %collective-permute-start.14 = (bf16[288,512]{1,0:T(8,128)(2,1)S(1)}, bf16[288,512]{1,0:T(8,128)(2,1)S(1)}, u32[]{:S(2)}, u32[]{:S(2)}) collective-permute-start(bf16[288,512]{1,0:T(8,128)(2,1)S(1)} %collective-permute-done.7.refs_7_), channel_id=1, source_target_pairs={{0,8},{8,0},{1,9},{9,1},{2,10},{10,2},{3,11},{11,3},{4,12},{12,4},... | collective-permute-start | bytes 884744 | tf_op jit(solution)/shard_map/ppermute | solution.py:294
  40.2 7.3 %collective-permute-start.16 = (bf16[288,512]{1,0:T(8,128)(2,1)S(1)}, bf16[288,512]{1,0:T(8,128)(2,1)S(1)}, u32[]{:S(2)}, u32[]{:S(2)}) collective-permute-start(bf16[288,512]{1,0:T(8,128)(2,1)S(1)} %collective-permute-done.9.refs_9_), channel_id=1, source_target_pairs={{0,8},{8,0},{1,9},{9,1},{2,10},{10,2},{3,11},{11,3},{4,12},{12,4},... | collective-permute-start | bytes 884744 | tf_op jit(solution)/shard_map/ppermute | solution.py:294
  40.3 7.2 %collective-permute-start.15 = (bf16[288,512]{1,0:T(8,128)(2,1)S(1)}, bf16[288,512]{1,0:T(8,128)(2,1)S(1)}, u32[]{:S(2)}, u32[]{:S(2)}) collective-permute-start(bf16[288,512]{1,0:T(8,128)(2,1)S(1)} %collective-permute-done.3.refs_8_), channel_id=1, source_target_pairs={{0,8},{8,0},{1,9},{9,1},{2,10},{10,2},{3,11},{11,3},{4,12},{12,4},... | collective-permute-start | bytes 884744 | tf_op jit(solution)/shard_map/ppermute | solution.py:294
  47.5 1.6 %collective-permute-start.17 = (bf16[288,512]{1,0:T(8,128)(2,1)S(1)}, bf16[288,512]{1,0:T(8,128)(2,1)S(1)}, u32[]{:S(2)}, u32[]{:S(2)}) collective-permute-start(bf16[288,512]{1,0:T(8,128)(2,1)S(1)} %collective-permute-done.10.refs_10_), channel_id=1, source_target_pairs={{0,8},{8,0},{1,9},{9,1},{2,10},{10,2},{3,11},{11,3},{4,12},{12,4},... | collective-permute-start | bytes 884744 | tf_op jit(solution)/shard_map/ppermute | solution.py:294
  51.5 4.7 %collective-permute-start.19 = (bf16[8,2,128,256]{3,2,1,0:T(8,128)(2,1)S(1)}, bf16[8,2,128,256]{3,2,1,0:T(8,128)(2,1)S(1)}, u32[]{:S(2)}, u32[]{:S(2)}) collective-permute-start(bf16[8,2,128,256]{3,2,1,0:T(8,128)(2,1)S(1)} %get-tuple-element.57), channel_id=1, source_target_pairs={{0,8},{8,0},{1,9},{9,1},{2,10},{10,2},{3,11},{11,3},{4,12},{12,4},... | collective-permute-start | bytes 3145736 | tf_op jit(solution)/shard_map/ppermute | solution.py:294
  51.9 3.1 %collective-permute-start.22 = (f32[16,128]{1,0:T(8,128)S(1)}, f32[16,128]{1,0:T(8,128)S(1)}, u32[]{:S(2)}, u32[]{:S(2)}) collective-permute-start(f32[16,128]{1,0:T(8,128)S(1)} %get-tuple-element.58), channel_id=1, source_target_pairs={{0,40},{8,32},{16,56},{24,48},{32,8},{40,0},{48,24},{56,16},{64,10... | collective-permute-start | bytes 24584 | tf_op jit(solution)/shard_map/ppermute | solution.py:308
  52.4 2.6 %collective-permute-start.21 = (f32[16,128]{1,0:T(8,128)S(1)}, f32[16,128]{1,0:T(8,128)S(1)}, u32[]{:S(2)}, u32[]{:S(2)}) collective-permute-start(f32[16,128]{1,0:T(8,128)S(1)} %get-tuple-element.58), channel_id=1, source_target_pairs={{0,8},{8,0},{16,24},{24,16},{32,40},{40,32},{48,56},{56,48},{64,72... | collective-permute-start | bytes 24584 | tf_op jit(solution)/shard_map/ppermute | solution.py:308
  52.5 3.7 %collective-permute-start.20 = (f32[16,128]{1,0:T(8,128)S(1)}, f32[16,128]{1,0:T(8,128)S(1)}, u32[]{:S(2)}, u32[]{:S(2)}) collective-permute-start(f32[16,128]{1,0:T(8,128)S(1)} %get-tuple-element.58), channel_id=1, source_target_pairs={{0,32},{8,40},{16,48},{24,56},{32,0},{40,8},{48,16},{56,24},{64,96... | collective-permute-start | bytes 24584 | tf_op jit(solution)/shard_map/ppermute | solution.py:308
  57.5 43.4 %all-to-all-start = ((bf16[16,128,256]{2,1,0:T(8,128)(2,1)}), bf16[16,128,256]{2,1,0:T(8,128)(2,1)S(1)}, u32[]{:S(2)}, u32[]{:S(2)}) async-start(bf16[16,128,256]{2,1,0:T(8,128)(2,1)} %bitcast.1), calls=%async_computation | async-start | bytes 2097152 | tf_op jit(solution)/shard_map/all_to_all | solution.py:360
  72.3 4.2 %collective-permute-start.25 = (f32[16,128]{1,0:T(8,128)S(1)}, f32[16,128]{1,0:T(8,128)S(1)}, u32[]{:S(2)}, u32[]{:S(2)}) collective-permute-start(f32[16,128]{1,0:T(8,128)S(1)} %add_add_fusion.3), channel_id=1, source_target_pairs={{0,6},{1,7},{2,4},{3,5},{4,2},{5,3},{6,0},{7,1},{8,14},{9,15},{10,... | collective-permute-start | bytes 24584 | tf_op jit(solution)/shard_map/ppermute | solution.py:308
  74.0 5.2 %collective-permute-start.24 = (f32[16,128]{1,0:T(8,128)S(1)}, f32[16,128]{1,0:T(8,128)S(1)}, u32[]{:S(2)}, u32[]{:S(2)}) collective-permute-start(f32[16,128]{1,0:T(8,128)S(1)} %add_add_fusion.3), channel_id=1, source_target_pairs={{0,4},{1,5},{2,6},{3,7},{4,0},{5,1},{6,2},{7,3},{8,12},{9,13},{10,... | collective-permute-start | bytes 24584 | tf_op jit(solution)/shard_map/ppermute | solution.py:308
  74.9 4.3 %collective-permute-start.23 = (f32[16,128]{1,0:T(8,128)S(1)}, f32[16,128]{1,0:T(8,128)S(1)}, u32[]{:S(2)}, u32[]{:S(2)}) collective-permute-start(f32[16,128]{1,0:T(8,128)S(1)} %add_add_fusion.3), channel_id=1, source_target_pairs={{0,2},{1,3},{2,0},{3,1},{4,6},{5,7},{6,4},{7,5},{8,10},{9,11},{10,... | collective-permute-start | bytes 24584 | tf_op jit(solution)/shard_map/ppermute | solution.py:308
  79.2 6.0 %collective-permute-start.28 = (f32[16,128]{1,0:T(8,128)S(1)}, f32[16,128]{1,0:T(8,128)S(1)}, u32[]{:S(2)}, u32[]{:S(2)}) collective-permute-start(f32[16,128]{1,0:T(8,128)S(1)} %add_add_fusion.2), channel_id=1, source_target_pairs={{0,17},{1,16},{2,19},{3,18},{4,21},{5,20},{6,23},{7,22},{16,1},{17... | collective-permute-start | bytes 24584 | tf_op jit(solution)/shard_map/ppermute | solution.py:308
  82.4 5.2 %collective-permute-start.27 = (f32[16,128]{1,0:T(8,128)S(1)}, f32[16,128]{1,0:T(8,128)S(1)}, u32[]{:S(2)}, u32[]{:S(2)}) collective-permute-start(f32[16,128]{1,0:T(8,128)S(1)} %add_add_fusion.2), channel_id=1, source_target_pairs={{0,1},{1,0},{2,3},{3,2},{4,5},{5,4},{6,7},{7,6},{16,17},{17,16},{1... | collective-permute-start | bytes 24584 | tf_op jit(solution)/shard_map/ppermute | solution.py:308
  83.2 4.4 %collective-permute-start.26 = (f32[16,128]{1,0:T(8,128)S(1)}, f32[16,128]{1,0:T(8,128)S(1)}, u32[]{:S(2)}, u32[]{:S(2)}) collective-permute-start(f32[16,128]{1,0:T(8,128)S(1)} %add_add_fusion.2), channel_id=1, source_target_pairs={{0,16},{1,17},{2,18},{3,19},{4,20},{5,21},{6,22},{7,23},{16,0},{17... | collective-permute-start | bytes 24584 | tf_op jit(solution)/shard_map/ppermute | solution.py:308
  83.4 10.8 %collective-permute-start.18 = (bf16[2,128,128]{2,1,0:T(8,128)(2,1)S(1)}, bf16[2,128,128]{2,1,0:T(8,128)(2,1)S(1)}, u32[]{:S(2)}, u32[]{:S(2)}) collective-permute-start(bf16[2,128,128]{2,1,0:T(8,128)(2,1)S(1)} %get-tuple-element.55), channel_id=1, source_target_pairs={{0,16},{16,0},{1,17},{17,1},{2,18},{18,2},{3,19},{19,3},{4,20},{20... | collective-permute-start | bytes 196616 | tf_op jit(solution)/shard_map/ppermute | solution.py:294
  87.6 11.2 %collective-permute-start.31 = (f32[16,128]{1,0:T(8,128)S(1)}, f32[16,128]{1,0:T(8,128)S(1)}, u32[]{:S(2)}, u32[]{:S(2)}) collective-permute-start(f32[16,128]{1,0:T(8,128)S(1)} %add_add_fusion.1), channel_id=1, source_target_pairs={{0,192},{32,224},{64,128},{96,160},{128,64},{160,96},{192,0},{224,... | collective-permute-start | bytes 24584 | tf_op jit(solution)/shard_map/ppermute | solution.py:308
  91.3 9.6 %collective-permute-start.30 = (f32[16,128]{1,0:T(8,128)S(1)}, f32[16,128]{1,0:T(8,128)S(1)}, u32[]{:S(2)}, u32[]{:S(2)}) collective-permute-start(f32[16,128]{1,0:T(8,128)S(1)} %add_add_fusion.1), channel_id=1, source_target_pairs={{0,128},{32,160},{64,192},{96,224},{128,0},{160,32},{192,64},{224,... | collective-permute-start | bytes 24584 | tf_op jit(solution)/shard_map/ppermute | solution.py:308
  93.6 7.2 %collective-permute-start.29 = (f32[16,128]{1,0:T(8,128)S(1)}, f32[16,128]{1,0:T(8,128)S(1)}, u32[]{:S(2)}, u32[]{:S(2)}) collective-permute-start(f32[16,128]{1,0:T(8,128)S(1)} %add_add_fusion.1), channel_id=1, source_target_pairs={{0,64},{32,96},{64,0},{96,32},{128,192},{160,224},{192,128},{224,1... | collective-permute-start | bytes 24584 | tf_op jit(solution)/shard_map/ppermute | solution.py:308
  (2 other events, 42.2 us)

commit v3 on v2

--- a/solution.py
+++ b/solution.py
@@ -111,18 +111,19 @@
     return combine(x.reshape(x.shape[0] // 8, 8, x.shape[1]), axis=0)
 
 
-A0, B0, A1, B1, A2, B2, A3, B3, N4 = range(9)
-XA1, XB1, XA2, XB2, XA3, XB3, X4 = range(9, 16)
-NS = 16
-BLOCKS = ((A0, B0), (A1, B1), (A2, B2), (A3, B3), (N4, X4), (XA3, XB3), (XA2, XB2), (XA1, XB1))
+A0, B0, A1, B1, A2, B2, A3, B3, A4, B4 = range(10)
+XA1, XB1, XA2, XB2, XA3, XB3, XA4, XB4 = range(10, 18)
+NS = 18
+BLOCKS = ((A0, B0), (A1, B1), (A2, B2), (A3, B3), None, (XA3, XB3), (XA2, XB2), (XA1, XB1))
 
 
 def pieces_of(n):
+    if n == FAR:
+        return [(A4, 0), (B4, 0), (XA4, 0), (XB4, 0)]
     out = []
     for side in range(2):
         for at in BLOCKS[n]:
-            flip = at >= XA1
-            out.append((at, PIECE * (1 - side if flip else side)))
+            out.append((at, PIECE * (1 - side if at >= XA1 else side)))
     return out
 
 
@@ -170,7 +171,7 @@
     curv = jnp.concatenate(curv, axis=1)
 
     def scores_of(d, diagonal):
-        s = dot(keys(d, 0, 1), q_t[HD:, :])
+        s = dot(keys(d, 0, 1), q_t[HD:, :]) * SCALE2
         if diagonal:
             s = masked(s, xl, core)
         score[d] = s
@@ -179,13 +180,13 @@
 
     scores_of(0, True)
     before(lambda d: scores_of(d, False))
-    top = jnp.max(tops[...], axis=0, keepdims=True) * SCALE2
+    top = jnp.max(tops[...], axis=0, keepdims=True)
     stat[0:1, :] = top
 
     def forward(d, diagonal):
         values_t = keys(d, 2, 4).T
         slope = dot(keys(d, 0, 2), q_t[...])
-        e = jnp.exp2(score[d] * SCALE2 - stat[0:1, :])
+        e = jnp.exp2(score[d] - stat[0:1, :])
         f = e * slope
         part_v = dot(values_t, e.astype(BF))
         part_t = dot(values_t[:HD], f.astype(BF))
@@ -212,17 +213,17 @@
     stat[1:2, :] = stat[0:1, :] + jnp.log2(tot)
     stat[2:3, :] = jnp.sum(cot.astype(F32) * out, axis=0, keepdims=True)
     acc_t[...] = jnp.zeros((HD, MQ), F32)
-    doc_acc[...] = jnp.zeros((DR, HD), F32)
+    doc_acc[...] = jnp.zeros((DR, 2 * HD), F32)
 
     def by_document(hots, terms):
         hot = jnp.concatenate(hots, axis=1).astype(BF)
         high = terms.astype(BF)
         low = (terms - high.astype(F32)).astype(BF)
-        return dot(hot, high) + dot(hot, low)
+        return dot(hot, jnp.concatenate([high, low], axis=1))
 
     def backward(d):
         keys_t = keys(d, 0, 1).T
-        p = jnp.exp2(score[d] * SCALE2 - stat[1:2, :])
+        p = jnp.exp2(score[d] - stat[1:2, :])
         push = dot(keys(d, 2, 3), cot_t[...])
         g = (p * (push - stat[2:3, :])).astype(BF)
         acc_t[...] += dot(keys_t, g)
@@ -233,8 +234,6 @@
             for s in range(2):
                 at = side * CH + s * ROWS
                 to_xl = xl if s == 0 else 1 - xl
-                if d == FAR:
-                    to_xl = jnp.where(core == 0, to_xl, 1 - to_xl)
                 g_ref[z - place(d), to_xl, :, :HD] = gk[at : at + ROWS].astype(BF)
                 g_ref[z - place(d), to_xl, :, HD:] = gv[at : at + ROWS].astype(BF)
         doc_acc[...] += by_document([onehot(p) for p in pieces_of(d)], terms)
@@ -281,7 +280,7 @@
             pltpu.VMEM((8, MQ), F32),
             pltpu.VMEM((8, MQ), F32),
             pltpu.VMEM((8, MQ), F32),
-            pltpu.VMEM((DR, HD), F32),
+            pltpu.VMEM((DR, 2 * HD), F32),
         ],
         compiler_params=pltpu.CompilerParams(vmem_limit_bytes=VMEM_LIMIT),
         cost_estimate=pl.CostEstimate(
@@ -347,10 +346,10 @@
             crossed.append(swap(late_b, "c"))
             b.append(around(b[k]))
     crossed.append(swap(b[FAR - 1], "c"))
-    far = around(jnp.where(lax.axis_index("c") == 0, a[FAR - 1], b[FAR - 1]))
+    far = [around(x[FAR - 1][:PIECE]) for x in (a, b)]
     native = [x for pair in zip(a, b) for x in pair]
     gq_mine, gq_other, g_own, g_sib, doc, count = attention(
-        (q_mine, q_other), native + [far] + crossed + [swap(far, "c")]
+        (q_mine, q_other), native + far + crossed + [swap(x, "c") for x in far]
     )
 
     from_sibling = swap(g_sib, "c")

time: 103 us -> 101 us (0.981)
  waiting for transfers between devices: 45.4 us -> 43.5 us
    ppermute x7 -> x8, waiting for transfers between devices: 29 us -> 27.2 us  [around(): return lax.ppermute(x, ('z', 'c'), pairs)]
    ppermute x7 -> x8, starting transfers between devices: 4.01 us -> 4.27 us  [around(): return lax.ppermute(x, ('z', 'c'), pairs)]
    ppermute x13 -> x14, waiting for transfers between devices: 3.81 us -> 3.63 us  [swap(): return lax.ppermute(x, axis, [(0, 1), (1, 0)])]
    ppermute x13 -> x14, starting transfers between devices: 7.47 us -> 7.35 us  [swap(): return lax.ppermute(x, axis, [(0, 1), (1, 0)])]
  transfers between devices with their start and end apart: 33 -> 35, of which waited for: 17 -> 18; matrix products, arithmetic and copies ran while one was open for 1% -> 1% of each run, Pallas kernels for 4% -> 4%
where the time goes in v3:
time: 101 us
  waiting for transfers between devices  43.5 us (43%)
  starting transfers between devices  43.4 us (43%)
  Pallas kernels  10.3 us (10%)
  other arithmetic  2.88 us (3%)
    ppermute x8, waiting for transfers between devices, around(): return lax.ppermute(x, ('z', 'c'), pairs)  27.2 us
    ppermute x12, starting transfers between devices, sum_of_four(): lax.ppermute(x, axes, [(i, i ^ m) for i in range(size)])  17.1 us
    all_to_all x1, starting transfers between devices, on_device(): lax.all_to_all(part.reshape(2 * NZ, ROWS, 2 * HD), ('z', 'xl'), 0, 0, til...  14.6 us
    ppermute x12, waiting for transfers between devices, sum_of_four(): lax.ppermute(x, axes, [(i, i ^ m) for i in range(size)])  12.7 us
    pallas_call x4, Pallas kernels, whole_call(): pl.pallas_call(kernel, out_shape=out_shape, in_specs=[vmem] * len(arrays)...  7.71 us
    ppermute x14, starting transfers between devices, swap(): return lax.ppermute(x, axis, [(0, 1), (1, 0)])  7.35 us
    ppermute x8, starting transfers between devices, around(): return lax.ppermute(x, ('z', 'c'), pairs)  4.27 us
    ppermute x14, waiting for transfers between devices, swap(): return lax.ppermute(x, axis, [(0, 1), (1, 0)])  3.63 us
  transfers between devices with their start and end apart: 35, of which 18 were waited for; matrix products, arithmetic and copies ran while one was open for 1% of the time, Pallas kernels for 4%

profile of v3, /device:TPU:8, one launch (start us, length us, event | category | flops | bytes accessed | tf_op | source)
XLA Modules:
  0.0 100.8 jit_solution(10812561083114472169)
XLA Ops:
  0.6 2.7 %shard_map.111 = (bf16[144,512]{1,0:T(8,128)(2,1)}, bf16[144,512]{1,0:T(8,128)(2,1)}) custom-call(bf16[128,2,128]{2,1,0:T(2,128)(2,1)} %k.1, bf16[128,2,128]{2,1,0:T(2,128)(2,1)} %v.1, bf16[128,2,128]{2,1,0:T(2,128)(2,1)} %kt.1, bf16[128,2,128]{2,1,0:T(2,128)(2,1)} %vt.1, s32[1,128]{1,0:T(1,128)} %bitcast.2), custom_call_target="tpu_custom_call" | custom-call | bytes 1048576 | tf_op jit(solution)/shard_map/pallas_call | solution.py:35
  3.4 1.5 %collective-permute-start.4 = (bf16[144,512]{1,0:T(8,128)(2,1)}, bf16[144,512]{1,0:T(8,128)(2,1)S(1)}, u32[]{:S(2)}, u32[]{:S(2)}) collective-permute-start(bf16[144,512]{1,0:T(8,128)(2,1)} %get-tuple-element.39), channel_id=1, source_target_pairs={{0,16},{16,0},{1,17},{17,1},{2,18},{18,2},{3,19},{19,3},{4,20},{20... | collective-permute-start | bytes 442376 | tf_op jit(solution)/shard_map/ppermute | solution.py:293
  5.9 2.6 %shard_map.112 = (bf16[144,512]{1,0:T(8,128)(2,1)}, bf16[144,512]{1,0:T(8,128)(2,1)}) custom-call(bf16[128,4,128]{2,1,0:T(4,128)(2,1)} %q, bf16[128,4,128]{2,1,0:T(4,128)(2,1)} %qt.1, f32[4,128]{1,0:T(4,128)} %curv.1), custom_call_target="tpu_custom_call" | custom-call | bytes 1048576 | tf_op jit(solution)/shard_map/pallas_call | solution.py:35
  8.4 1.4 %collective-permute-done.4 = bf16[144,512]{1,0:T(8,128)(2,1)S(1)} collective-permute-done((bf16[144,512]{1,0:T(8,128)(2,1)}, bf16[144,512]{1,0:T(8,128)(2,1)S(1)}, u32[]{:S(2)}, u32[]{:S(2)}) %collective-permute-start.4) | collective-permute-done | bytes 147488 | tf_op jit(solution)/shard_map/ppermute | solution.py:293
  9.8 1.9 %collective-permute-start.1 = (bf16[288,512]{1,0:T(8,128)(2,1)S(1)}, bf16[288,512]{1,0:T(8,128)(2,1)S(1)}, u32[]{:S(2)}, u32[]{:S(2)}) collective-permute-start(bf16[288,512]{1,0:T(8,128)(2,1)S(1)} %pad_maximum_fusion.refs_2_), channel_id=1, source_target_pairs={{0,32},{8,232},{32,64},{40,8},{64,96},{72,40},{96,128},{104,72},{1... | collective-permute-start | bytes 884744 | tf_op jit(solution)/shard_map/ppermute | solution.py:298
  11.8 2.0 %collective-permute-start.6 = (bf16[288,512]{1,0:T(8,128)(2,1)S(1)}, bf16[288,512]{1,0:T(8,128)(2,1)S(1)}, u32[]{:S(2)}, u32[]{:S(2)}) collective-permute-start(bf16[288,512]{1,0:T(8,128)(2,1)S(1)} %constant_dynamic-update-slice_fusion.refs_3_), channel_id=1, source_target_pairs={{0,32},{8,232},{32,64},{40,8},{64,96},{72,40},{96,128},{104,72},{1... | collective-permute-start | bytes 884744 | tf_op jit(solution)/shard_map/ppermute | solution.py:298
  13.8 6.6 %collective-permute-done.1.refs_4_ = bf16[288,512]{1,0:T(8,128)(2,1)S(1)} collective-permute-done((bf16[288,512]{1,0:T(8,128)(2,1)S(1)}, bf16[288,512]{1,0:T(8,128)(2,1)S(1)}, u32[]{:S(2)}, u32[]{:S(2)}) %collective-permute-start.1) | collective-permute-done | bytes 294944 | tf_op jit(solution)/shard_map/ppermute | solution.py:298
  20.4 3.2 %collective-permute-done.6.refs_5_ = bf16[288,512]{1,0:T(8,128)(2,1)S(1)} collective-permute-done((bf16[288,512]{1,0:T(8,128)(2,1)S(1)}, bf16[288,512]{1,0:T(8,128)(2,1)S(1)}, u32[]{:S(2)}, u32[]{:S(2)}) %collective-permute-start.6) | collective-permute-done | bytes 294944 | tf_op jit(solution)/shard_map/ppermute | solution.py:298
  23.5 1.5 %collective-permute-start.8 = (bf16[144,512]{1,0:T(8,128)(2,1)}, bf16[144,512]{1,0:T(8,128)(2,1)S(1)}, u32[]{:S(2)}, u32[]{:S(2)}) collective-permute-start(bf16[144,512]{1,0:T(8,128)(2,1)} %get-tuple-element.44), channel_id=1, source_target_pairs={{0,16},{16,0},{1,17},{17,1},{2,18},{18,2},{3,19},{19,3},{4,20},{20... | collective-permute-start | bytes 442376 | tf_op jit(solution)/shard_map/ppermute | solution.py:293
  25.0 3.3 %collective-permute-done.2.refs_6_ = bf16[288,512]{1,0:T(8,128)(2,1)S(1)} collective-permute-done((bf16[288,512]{1,0:T(8,128)(2,1)S(1)}, bf16[288,512]{1,0:T(8,128)(2,1)S(1)}, u32[]{:S(2)}, u32[]{:S(2)}) %collective-permute-start.2) | collective-permute-done | bytes 294944 | tf_op jit(solution)/shard_map/ppermute | solution.py:298
  29.1 2.4 %collective-permute-done.7.refs_7_ = bf16[288,512]{1,0:T(8,128)(2,1)S(1)} collective-permute-done((bf16[288,512]{1,0:T(8,128)(2,1)S(1)}, bf16[288,512]{1,0:T(8,128)(2,1)S(1)}, u32[]{:S(2)}, u32[]{:S(2)}) %collective-permute-start.7) | collective-permute-done | bytes 294944 | tf_op jit(solution)/shard_map/ppermute | solution.py:298
  33.2 3.1 %collective-permute-done.3.refs_8_ = bf16[288,512]{1,0:T(8,128)(2,1)S(1)} collective-permute-done((bf16[288,512]{1,0:T(8,128)(2,1)S(1)}, bf16[288,512]{1,0:T(8,128)(2,1)S(1)}, u32[]{:S(2)}, u32[]{:S(2)}) %collective-permute-start.3) | collective-permute-done | bytes 294944 | tf_op jit(solution)/shard_map/ppermute | solution.py:298
  36.4 3.1 %collective-permute-done.9.refs_9_ = bf16[288,512]{1,0:T(8,128)(2,1)S(1)} collective-permute-done((bf16[288,512]{1,0:T(8,128)(2,1)S(1)}, bf16[288,512]{1,0:T(8,128)(2,1)S(1)}, u32[]{:S(2)}, u32[]{:S(2)}) %collective-permute-start.9) | collective-permute-done | bytes 294944 | tf_op jit(solution)/shard_map/ppermute | solution.py:298
  40.4 2.3 %collective-permute-done.10.refs_10_ = bf16[144,512]{1,0:T(8,128)(2,1)S(1)} collective-permute-done((bf16[144,512]{1,0:T(8,128)(2,1)S(1)}, bf16[144,512]{1,0:T(8,128)(2,1)S(1)}, u32[]{:S(2)}, u32[]{:S(2)}) %collective-permute-start.10) | collective-permute-done | bytes 147488 | tf_op jit(solution)/shard_map/ppermute | solution.py:298
  42.7 3.4 %collective-permute-done.11.refs_11_ = bf16[144,512]{1,0:T(8,128)(2,1)S(1)} collective-permute-done((bf16[144,512]{1,0:T(8,128)(2,1)S(1)}, bf16[144,512]{1,0:T(8,128)(2,1)S(1)}, u32[]{:S(2)}, u32[]{:S(2)}) %collective-permute-start.11) | collective-permute-done | bytes 147488 | tf_op jit(solution)/shard_map/ppermute | solution.py:298
  46.1 1.4 %collective-permute-done.19.refs_19_ = bf16[144,512]{1,0:T(8,128)(2,1)S(1)} collective-permute-done((bf16[144,512]{1,0:T(8,128)(2,1)S(1)}, bf16[144,512]{1,0:T(8,128)(2,1)S(1)}, u32[]{:S(2)}, u32[]{:S(2)}) %collective-permute-start.19) | collective-permute-done | bytes 147488 | tf_op jit(solution)/shard_map/ppermute | solution.py:293
  47.4 2.6 %shard_map.113 = (bf16[2,128,128]{2,1,0:T(8,128)(2,1)S(1)}, bf16[2,128,128]{2,1,0:T(8,128)(2,1)S(1)}, bf16[8,2,128,256]{3,2,1,0:T(8,128)(2,1)S(1)}, bf16[8,2,128...) custom-call(bf16[144,512]{1,0:T(8,128)(2,1)S(1)} %copy-done, ...), custom_call_target="tpu_custom_call" | custom-call | flops 8589934592 | bytes 8388608 | tf_op jit(solution)/shard_map/pallas_call | solution.py:266
  50.8 1.5 %collective-permute-start.22 = (f32[16,128]{1,0:T(8,128)S(1)}, f32[16,128]{1,0:T(8,128)S(1)}, u32[]{:S(2)}, u32[]{:S(2)}) collective-permute-start(f32[16,128]{1,0:T(8,128)S(1)} %get-tuple-element.58), channel_id=1, source_target_pairs={{0,32},{8,40},{16,48},{24,56},{32,0},{40,8},{48,16},{56,24},{64,96... | collective-permute-start | bytes 24584 | tf_op jit(solution)/shard_map/ppermute | solution.py:307
  54.4 1.3 %add_convert_fusion = bf16[8,2,128,256]{3,2,1,0:T(8,128)(2,1)} fusion(bf16[8,2,128,256]{3,2,1,0:T(8,128)(2,1)S(1)} %collective-permute-done.21, bf16[8,2,128,256]{3,2,1,0:T(8,128)(2,1)S(1)} %get-tuple-element.56), kind=kLoop, calls=%fused_computation | loop fusion | flops 2097152 | bytes 3145728 | tf_op jit(solution)/shard_map/convert_element_type | solution.py:357
  55.7 14.6 %all-to-all-start = ((bf16[16,128,256]{2,1,0:T(8,128)(2,1)}), bf16[16,128,256]{2,1,0:T(8,128)(2,1)S(1)}, u32[]{:S(2)}, u32[]{:S(2)}) async-start(bf16[16,128,256]{2,1,0:T(8,128)(2,1)} %bitcast.1), calls=%async_computation | async-start | bytes 2097152 | tf_op jit(solution)/shard_map/all_to_all | solution.py:359
  70.4 1.6 %collective-permute-start.27 = (f32[16,128]{1,0:T(8,128)S(1)}, f32[16,128]{1,0:T(8,128)S(1)}, u32[]{:S(2)}, u32[]{:S(2)}) collective-permute-start(f32[16,128]{1,0:T(8,128)S(1)} %add_add_fusion.3), channel_id=1, source_target_pairs={{0,6},{1,7},{2,4},{3,5},{4,2},{5,3},{6,0},{7,1},{8,14},{9,15},{10,... | collective-permute-start | bytes 24584 | tf_op jit(solution)/shard_map/ppermute | solution.py:307
  73.0 1.6 %collective-permute-start.25 = (f32[16,128]{1,0:T(8,128)S(1)}, f32[16,128]{1,0:T(8,128)S(1)}, u32[]{:S(2)}, u32[]{:S(2)}) collective-permute-start(f32[16,128]{1,0:T(8,128)S(1)} %add_add_fusion.3), channel_id=1, source_target_pairs={{0,2},{1,3},{2,0},{3,1},{4,6},{5,7},{6,4},{7,5},{8,10},{9,11},{10,... | collective-permute-start | bytes 24584 | tf_op jit(solution)/shard_map/ppermute | solution.py:307
  74.6 2.6 %collective-permute-done.26 = f32[16,128]{1,0:T(8,128)S(1)} collective-permute-done((f32[16,128]{1,0:T(8,128)S(1)}, f32[16,128]{1,0:T(8,128)S(1)}, u32[]{:S(2)}, u32[]{:S(2)}) %collective-permute-start.26) | collective-permute-done | bytes 8224 | tf_op jit(solution)/shard_map/ppermute | solution.py:307
  77.2 3.2 %collective-permute-start.30 = (f32[16,128]{1,0:T(8,128)S(1)}, f32[16,128]{1,0:T(8,128)S(1)}, u32[]{:S(2)}, u32[]{:S(2)}) collective-permute-start(f32[16,128]{1,0:T(8,128)S(1)} %add_add_fusion.2), channel_id=1, source_target_pairs={{0,17},{1,16},{2,19},{3,18},{4,21},{5,20},{6,23},{7,22},{16,1},{17... | collective-permute-start | bytes 24584 | tf_op jit(solution)/shard_map/ppermute | solution.py:307
  81.4 1.8 %collective-permute-start.20 = (bf16[2,128,128]{2,1,0:T(8,128)(2,1)S(1)}, bf16[2,128,128]{2,1,0:T(8,128)(2,1)S(1)}, u32[]{:S(2)}, u32[]{:S(2)}) collective-permute-start(bf16[2,128,128]{2,1,0:T(8,128)(2,1)S(1)} %get-tuple-element.55), channel_id=1, source_target_pairs={{0,16},{16,0},{1,17},{17,1},{2,18},{18,2},{3,19},{19,3},{4,20},{20... | collective-permute-start | bytes 196616 | tf_op jit(solution)/shard_map/ppermute | solution.py:293
  83.2 2.4 %collective-permute-done.29 = f32[16,128]{1,0:T(8,128)S(1)} collective-permute-done((f32[16,128]{1,0:T(8,128)S(1)}, f32[16,128]{1,0:T(8,128)S(1)}, u32[]{:S(2)}, u32[]{:S(2)}) %collective-permute-start.29) | collective-permute-done | bytes 8224 | tf_op jit(solution)/shard_map/ppermute | solution.py:307
  85.6 3.6 %collective-permute-start.33 = (f32[16,128]{1,0:T(8,128)S(1)}, f32[16,128]{1,0:T(8,128)S(1)}, u32[]{:S(2)}, u32[]{:S(2)}) collective-permute-start(f32[16,128]{1,0:T(8,128)S(1)} %add_add_fusion.1), channel_id=1, source_target_pairs={{0,192},{32,224},{64,128},{96,160},{128,64},{160,96},{192,0},{224,... | collective-permute-start | bytes 24584 | tf_op jit(solution)/shard_map/ppermute | solution.py:307
  89.2 2.4 %collective-permute-start.32 = (f32[16,128]{1,0:T(8,128)S(1)}, f32[16,128]{1,0:T(8,128)S(1)}, u32[]{:S(2)}, u32[]{:S(2)}) collective-permute-start(f32[16,128]{1,0:T(8,128)S(1)} %add_add_fusion.1), channel_id=1, source_target_pairs={{0,128},{32,160},{64,192},{96,224},{128,0},{160,32},{192,64},{224,... | collective-permute-start | bytes 24584 | tf_op jit(solution)/shard_map/ppermute | solution.py:307
  92.2 1.2 %shard_map.114 = bf16[128,4,128]{2,1,0:T(4,128)(2,1)} custom-call(bf16[2,128,128]{2,1,0:T(8,128)(2,1)S(1)} %get-tuple-element.54.mine, bf16[2,128,128]{2,1,0:T(8,128)(2,1)S(1)} %collective-permute-done.20.other), custom_call_target="tpu_custom_call" | custom-call | bytes 1048576 | tf_op jit(solution)/shard_map/pallas_call | solution.py:35
  93.4 3.5 %collective-permute-done.33 = f32[16,128]{1,0:T(8,128)S(1)} collective-permute-done((f32[16,128]{1,0:T(8,128)S(1)}, f32[16,128]{1,0:T(8,128)S(1)}, u32[]{:S(2)}, u32[]{:S(2)}) %collective-permute-start.33) | collective-permute-done | bytes 8224 | tf_op jit(solution)/shard_map/ppermute | solution.py:307
  96.9 2.1 %collective-permute-done.32 = f32[16,128]{1,0:T(8,128)S(1)} collective-permute-done((f32[16,128]{1,0:T(8,128)S(1)}, f32[16,128]{1,0:T(8,128)S(1)}, u32[]{:S(2)}, u32[]{:S(2)}) %collective-permute-start.32) | collective-permute-done | bytes 8224 | tf_op jit(solution)/shard_map/ppermute | solution.py:307
  99.0 1.2 %shard_map.115 = (bf16[128,2,128]{2,1,0:T(2,128)(2,1)}, bf16[128,2,128]{2,1,0:T(2,128)(2,1)}) custom-call(bf16[16,128,256]{2,1,0:T(8,128)(2,1)S(1)} %all-to-all-done.parts), custom_call_target="tpu_custom_call" | custom-call | bytes 1048576 | tf_op jit(solution)/shard_map/pallas_call | solution.py:35
  (56 shorter events, 10.7 us)
Async XLA Ops:
  3.4 6.5 %collective-permute-start.4 = (bf16[144,512]{1,0:T(8,128)(2,1)}, bf16[144,512]{1,0:T(8,128)(2,1)S(1)}, u32[]{:S(2)}, u32[]{:S(2)}) collective-permute-start(bf16[144,512]{1,0:T(8,128)(2,1)} %get-tuple-element.39), channel_id=1, source_target_pairs={{0,16},{16,0},{1,17},{17,1},{2,18},{18,2},{3,19},{19,3},{4,20},{20... | collective-permute-start | bytes 442376 | tf_op jit(solution)/shard_map/ppermute | solution.py:293
  9.8 10.6 %collective-permute-start.1 = (bf16[288,512]{1,0:T(8,128)(2,1)S(1)}, bf16[288,512]{1,0:T(8,128)(2,1)S(1)}, u32[]{:S(2)}, u32[]{:S(2)}) collective-permute-start(bf16[288,512]{1,0:T(8,128)(2,1)S(1)} %pad_maximum_fusion.refs_2_), channel_id=1, source_target_pairs={{0,32},{8,232},{32,64},{40,8},{64,96},{72,40},{96,128},{104,72},{1... | collective-permute-start | bytes 884744 | tf_op jit(solution)/shard_map/ppermute | solution.py:298
  11.8 11.8 %collective-permute-start.6 = (bf16[288,512]{1,0:T(8,128)(2,1)S(1)}, bf16[288,512]{1,0:T(8,128)(2,1)S(1)}, u32[]{:S(2)}, u32[]{:S(2)}) collective-permute-start(bf16[288,512]{1,0:T(8,128)(2,1)S(1)} %constant_dynamic-update-slice_fusion.refs_3_), channel_id=1, source_target_pairs={{0,32},{8,232},{32,64},{40,8},{64,96},{72,40},{96,128},{104,72},{1... | collective-permute-start | bytes 884744 | tf_op jit(solution)/shard_map/ppermute | solution.py:298
  20.4 7.9 %collective-permute-start.2 = (bf16[288,512]{1,0:T(8,128)(2,1)S(1)}, bf16[288,512]{1,0:T(8,128)(2,1)S(1)}, u32[]{:S(2)}, u32[]{:S(2)}) collective-permute-start(bf16[288,512]{1,0:T(8,128)(2,1)S(1)} %collective-permute-done.1.refs_4_), channel_id=1, source_target_pairs={{0,32},{8,232},{32,64},{40,8},{64,96},{72,40},{96,128},{104,72},{1... | collective-permute-start | bytes 884744 | tf_op jit(solution)/shard_map/ppermute | solution.py:298
  23.5 7.9 %collective-permute-start.7 = (bf16[288,512]{1,0:T(8,128)(2,1)S(1)}, bf16[288,512]{1,0:T(8,128)(2,1)S(1)}, u32[]{:S(2)}, u32[]{:S(2)}) collective-permute-start(bf16[288,512]{1,0:T(8,128)(2,1)S(1)} %collective-permute-done.6.refs_5_), channel_id=1, source_target_pairs={{0,32},{8,232},{32,64},{40,8},{64,96},{72,40},{96,128},{104,72},{1... | collective-permute-start | bytes 884744 | tf_op jit(solution)/shard_map/ppermute | solution.py:298
  23.5 5.6 %collective-permute-start.8 = (bf16[144,512]{1,0:T(8,128)(2,1)}, bf16[144,512]{1,0:T(8,128)(2,1)S(1)}, u32[]{:S(2)}, u32[]{:S(2)}) collective-permute-start(bf16[144,512]{1,0:T(8,128)(2,1)} %get-tuple-element.44), channel_id=1, source_target_pairs={{0,16},{16,0},{1,17},{17,1},{2,18},{18,2},{3,19},{19,3},{4,20},{20... | collective-permute-start | bytes 442376 | tf_op jit(solution)/shard_map/ppermute | solution.py:293
  28.3 7.9 %collective-permute-start.3 = (bf16[288,512]{1,0:T(8,128)(2,1)S(1)}, bf16[288,512]{1,0:T(8,128)(2,1)S(1)}, u32[]{:S(2)}, u32[]{:S(2)}) collective-permute-start(bf16[288,512]{1,0:T(8,128)(2,1)S(1)} %collective-permute-done.2.refs_6_), channel_id=1, source_target_pairs={{0,32},{8,232},{32,64},{40,8},{64,96},{72,40},{96,128},{104,72},{1... | collective-permute-start | bytes 884744 | tf_op jit(solution)/shard_map/ppermute | solution.py:298
  31.5 7.9 %collective-permute-start.9 = (bf16[288,512]{1,0:T(8,128)(2,1)S(1)}, bf16[288,512]{1,0:T(8,128)(2,1)S(1)}, u32[]{:S(2)}, u32[]{:S(2)}) collective-permute-start(bf16[288,512]{1,0:T(8,128)(2,1)S(1)} %collective-permute-done.7.refs_7_), channel_id=1, source_target_pairs={{0,32},{8,232},{32,64},{40,8},{64,96},{72,40},{96,128},{104,72},{1... | collective-permute-start | bytes 884744 | tf_op jit(solution)/shard_map/ppermute | solution.py:298
  31.5 8.0 %collective-permute-start.12 = (bf16[288,512]{1,0:T(8,128)(2,1)S(1)}, bf16[288,512]{1,0:T(8,128)(2,1)S(1)}, u32[]{:S(2)}, u32[]{:S(2)}) collective-permute-start(bf16[288,512]{1,0:T(8,128)(2,1)S(1)} %collective-permute-done.1.refs_4_), channel_id=1, source_target_pairs={{0,8},{8,0},{1,9},{9,1},{2,10},{10,2},{3,11},{11,3},{4,12},{12,4},... | collective-permute-start | bytes 884744 | tf_op jit(solution)/shard_map/ppermute | solution.py:293
  32.6 7.1 %collective-permute-start.13 = (bf16[288,512]{1,0:T(8,128)(2,1)S(1)}, bf16[288,512]{1,0:T(8,128)(2,1)S(1)}, u32[]{:S(2)}, u32[]{:S(2)}) collective-permute-start(bf16[288,512]{1,0:T(8,128)(2,1)S(1)} %collective-permute-done.6.refs_5_), channel_id=1, source_target_pairs={{0,8},{8,0},{1,9},{9,1},{2,10},{10,2},{3,11},{11,3},{4,12},{12,4},... | collective-permute-start | bytes 884744 | tf_op jit(solution)/shard_map/ppermute | solution.py:293
  32.6 7.7 %collective-permute-start.14 = (bf16[288,512]{1,0:T(8,128)(2,1)S(1)}, bf16[288,512]{1,0:T(8,128)(2,1)S(1)}, u32[]{:S(2)}, u32[]{:S(2)}) collective-permute-start(bf16[288,512]{1,0:T(8,128)(2,1)S(1)} %collective-permute-done.2.refs_6_), channel_id=1, source_target_pairs={{0,8},{8,0},{1,9},{9,1},{2,10},{10,2},{3,11},{11,3},{4,12},{12,4},... | collective-permute-start | bytes 884744 | tf_op jit(solution)/shard_map/ppermute | solution.py:293
  36.3 6.4 %collective-permute-start.10 = (bf16[144,512]{1,0:T(8,128)(2,1)S(1)}, bf16[144,512]{1,0:T(8,128)(2,1)S(1)}, u32[]{:S(2)}, u32[]{:S(2)}) collective-permute-start(bf16[144,512]{1,0:T(8,128)(2,1)S(1)} %slice.16), channel_id=1, source_target_pairs={{0,32},{8,232},{32,64},{40,8},{64,96},{72,40},{96,128},{104,72},{1... | collective-permute-start | bytes 442376 | tf_op jit(solution)/shard_map/ppermute | solution.py:298
  39.4 6.7 %collective-permute-start.15 = (bf16[288,512]{1,0:T(8,128)(2,1)S(1)}, bf16[288,512]{1,0:T(8,128)(2,1)S(1)}, u32[]{:S(2)}, u32[]{:S(2)}) collective-permute-start(bf16[288,512]{1,0:T(8,128)(2,1)S(1)} %collective-permute-done.7.refs_7_), channel_id=1, source_target_pairs={{0,8},{8,0},{1,9},{9,1},{2,10},{10,2},{3,11},{11,3},{4,12},{12,4},... | collective-permute-start | bytes 884744 | tf_op jit(solution)/shard_map/ppermute | solution.py:293
  39.4 6.6 %collective-permute-start.11 = (bf16[144,512]{1,0:T(8,128)(2,1)S(1)}, bf16[144,512]{1,0:T(8,128)(2,1)S(1)}, u32[]{:S(2)}, u32[]{:S(2)}) collective-permute-start(bf16[144,512]{1,0:T(8,128)(2,1)S(1)} %slice.13), channel_id=1, source_target_pairs={{0,32},{8,232},{32,64},{40,8},{64,96},{72,40},{96,128},{104,72},{1... | collective-permute-start | bytes 442376 | tf_op jit(solution)/shard_map/ppermute | solution.py:298
  39.7 7.7 %collective-permute-start.16 = (bf16[288,512]{1,0:T(8,128)(2,1)S(1)}, bf16[288,512]{1,0:T(8,128)(2,1)S(1)}, u32[]{:S(2)}, u32[]{:S(2)}) collective-permute-start(bf16[288,512]{1,0:T(8,128)(2,1)S(1)} %collective-permute-done.3.refs_8_), channel_id=1, source_target_pairs={{0,8},{8,0},{1,9},{9,1},{2,10},{10,2},{3,11},{11,3},{4,12},{12,4},... | collective-permute-start | bytes 884744 | tf_op jit(solution)/shard_map/ppermute | solution.py:293
  40.3 7.1 %collective-permute-start.17 = (bf16[288,512]{1,0:T(8,128)(2,1)S(1)}, bf16[288,512]{1,0:T(8,128)(2,1)S(1)}, u32[]{:S(2)}, u32[]{:S(2)}) collective-permute-start(bf16[288,512]{1,0:T(8,128)(2,1)S(1)} %collective-permute-done.9.refs_9_), channel_id=1, source_target_pairs={{0,8},{8,0},{1,9},{9,1},{2,10},{10,2},{3,11},{11,3},{4,12},{12,4},... | collective-permute-start | bytes 884744 | tf_op jit(solution)/shard_map/ppermute | solution.py:293
  42.7 3.4 %collective-permute-start.18 = (bf16[144,512]{1,0:T(8,128)(2,1)S(1)}, bf16[144,512]{1,0:T(8,128)(2,1)S(1)}, u32[]{:S(2)}, u32[]{:S(2)}) collective-permute-start(bf16[144,512]{1,0:T(8,128)(2,1)S(1)} %collective-permute-done.10.refs_10_), channel_id=1, source_target_pairs={{0,8},{8,0},{1,9},{9,1},{2,10},{10,2},{3,11},{11,3},{4,12},{12,4},... | collective-permute-start | bytes 442376 | tf_op jit(solution)/shard_map/ppermute | solution.py:293
  50.0 4.4 %collective-permute-start.21 = (bf16[8,2,128,256]{3,2,1,0:T(8,128)(2,1)S(1)}, bf16[8,2,128,256]{3,2,1,0:T(8,128)(2,1)S(1)}, u32[]{:S(2)}, u32[]{:S(2)}) collective-permute-start(bf16[8,2,128,256]{3,2,1,0:T(8,128)(2,1)S(1)} %get-tuple-element.57), channel_id=1, source_target_pairs={{0,8},{8,0},{1,9},{9,1},{2,10},{10,2},{3,11},{11,3},{4,12},{12,4},... | collective-permute-start | bytes 3145736 | tf_op jit(solution)/shard_map/ppermute | solution.py:293
  50.2 3.1 %collective-permute-start.24 = (f32[16,128]{1,0:T(8,128)S(1)}, f32[16,128]{1,0:T(8,128)S(1)}, u32[]{:S(2)}, u32[]{:S(2)}) collective-permute-start(f32[16,128]{1,0:T(8,128)S(1)} %get-tuple-element.58), channel_id=1, source_target_pairs={{0,40},{8,32},{16,56},{24,48},{32,8},{40,0},{48,24},{56,16},{64,10... | collective-permute-start | bytes 24584 | tf_op jit(solution)/shard_map/ppermute | solution.py:307
  50.6 2.6 %collective-permute-start.23 = (f32[16,128]{1,0:T(8,128)S(1)}, f32[16,128]{1,0:T(8,128)S(1)}, u32[]{:S(2)}, u32[]{:S(2)}) collective-permute-start(f32[16,128]{1,0:T(8,128)S(1)} %get-tuple-element.58), channel_id=1, source_target_pairs={{0,8},{8,0},{16,24},{24,16},{32,40},{40,32},{48,56},{56,48},{64,72... | collective-permute-start | bytes 24584 | tf_op jit(solution)/shard_map/ppermute | solution.py:307
  50.8 3.7 %collective-permute-start.22 = (f32[16,128]{1,0:T(8,128)S(1)}, f32[16,128]{1,0:T(8,128)S(1)}, u32[]{:S(2)}, u32[]{:S(2)}) collective-permute-start(f32[16,128]{1,0:T(8,128)S(1)} %get-tuple-element.58), channel_id=1, source_target_pairs={{0,32},{8,40},{16,48},{24,56},{32,0},{40,8},{48,16},{56,24},{64,96... | collective-permute-start | bytes 24584 | tf_op jit(solution)/shard_map/ppermute | solution.py:307
  55.7 43.2 %all-to-all-start = ((bf16[16,128,256]{2,1,0:T(8,128)(2,1)}), bf16[16,128,256]{2,1,0:T(8,128)(2,1)S(1)}, u32[]{:S(2)}, u32[]{:S(2)}) async-start(bf16[16,128,256]{2,1,0:T(8,128)(2,1)} %bitcast.1), calls=%async_computation | async-start | bytes 2097152 | tf_op jit(solution)/shard_map/all_to_all | solution.py:359
  70.4 4.2 %collective-permute-start.27 = (f32[16,128]{1,0:T(8,128)S(1)}, f32[16,128]{1,0:T(8,128)S(1)}, u32[]{:S(2)}, u32[]{:S(2)}) collective-permute-start(f32[16,128]{1,0:T(8,128)S(1)} %add_add_fusion.3), channel_id=1, source_target_pairs={{0,6},{1,7},{2,4},{3,5},{4,2},{5,3},{6,0},{7,1},{8,14},{9,15},{10,... | collective-permute-start | bytes 24584 | tf_op jit(solution)/shard_map/ppermute | solution.py:307
  72.0 5.2 %collective-permute-start.26 = (f32[16,128]{1,0:T(8,128)S(1)}, f32[16,128]{1,0:T(8,128)S(1)}, u32[]{:S(2)}, u32[]{:S(2)}) collective-permute-start(f32[16,128]{1,0:T(8,128)S(1)} %add_add_fusion.3), channel_id=1, source_target_pairs={{0,4},{1,5},{2,6},{3,7},{4,0},{5,1},{6,2},{7,3},{8,12},{9,13},{10,... | collective-permute-start | bytes 24584 | tf_op jit(solution)/shard_map/ppermute | solution.py:307
  73.0 4.2 %collective-permute-start.25 = (f32[16,128]{1,0:T(8,128)S(1)}, f32[16,128]{1,0:T(8,128)S(1)}, u32[]{:S(2)}, u32[]{:S(2)}) collective-permute-start(f32[16,128]{1,0:T(8,128)S(1)} %add_add_fusion.3), channel_id=1, source_target_pairs={{0,2},{1,3},{2,0},{3,1},{4,6},{5,7},{6,4},{7,5},{8,10},{9,11},{10,... | collective-permute-start | bytes 24584 | tf_op jit(solution)/shard_map/ppermute | solution.py:307
  77.2 6.0 %collective-permute-start.30 = (f32[16,128]{1,0:T(8,128)S(1)}, f32[16,128]{1,0:T(8,128)S(1)}, u32[]{:S(2)}, u32[]{:S(2)}) collective-permute-start(f32[16,128]{1,0:T(8,128)S(1)} %add_add_fusion.2), channel_id=1, source_target_pairs={{0,17},{1,16},{2,19},{3,18},{4,21},{5,20},{6,23},{7,22},{16,1},{17... | collective-permute-start | bytes 24584 | tf_op jit(solution)/shard_map/ppermute | solution.py:307
  80.4 5.2 %collective-permute-start.29 = (f32[16,128]{1,0:T(8,128)S(1)}, f32[16,128]{1,0:T(8,128)S(1)}, u32[]{:S(2)}, u32[]{:S(2)}) collective-permute-start(f32[16,128]{1,0:T(8,128)S(1)} %add_add_fusion.2), channel_id=1, source_target_pairs={{0,1},{1,0},{2,3},{3,2},{4,5},{5,4},{6,7},{7,6},{16,17},{17,16},{1... | collective-permute-start | bytes 24584 | tf_op jit(solution)/shard_map/ppermute | solution.py:307
  81.2 4.4 %collective-permute-start.28 = (f32[16,128]{1,0:T(8,128)S(1)}, f32[16,128]{1,0:T(8,128)S(1)}, u32[]{:S(2)}, u32[]{:S(2)}) collective-permute-start(f32[16,128]{1,0:T(8,128)S(1)} %add_add_fusion.2), channel_id=1, source_target_pairs={{0,16},{1,17},{2,18},{3,19},{4,20},{5,21},{6,22},{7,23},{16,0},{17... | collective-permute-start | bytes 24584 | tf_op jit(solution)/shard_map/ppermute | solution.py:307
  81.4 10.8 %collective-permute-start.20 = (bf16[2,128,128]{2,1,0:T(8,128)(2,1)S(1)}, bf16[2,128,128]{2,1,0:T(8,128)(2,1)S(1)}, u32[]{:S(2)}, u32[]{:S(2)}) collective-permute-start(bf16[2,128,128]{2,1,0:T(8,128)(2,1)S(1)} %get-tuple-element.55), channel_id=1, source_target_pairs={{0,16},{16,0},{1,17},{17,1},{2,18},{18,2},{3,19},{19,3},{4,20},{20... | collective-permute-start | bytes 196616 | tf_op jit(solution)/shard_map/ppermute | solution.py:293
  85.6 11.3 %collective-permute-start.33 = (f32[16,128]{1,0:T(8,128)S(1)}, f32[16,128]{1,0:T(8,128)S(1)}, u32[]{:S(2)}, u32[]{:S(2)}) collective-permute-start(f32[16,128]{1,0:T(8,128)S(1)} %add_add_fusion.1), channel_id=1, source_target_pairs={{0,192},{32,224},{64,128},{96,160},{128,64},{160,96},{192,0},{224,... | collective-permute-start | bytes 24584 | tf_op jit(solution)/shard_map/ppermute | solution.py:307
  89.2 9.7 %collective-permute-start.32 = (f32[16,128]{1,0:T(8,128)S(1)}, f32[16,128]{1,0:T(8,128)S(1)}, u32[]{:S(2)}, u32[]{:S(2)}) collective-permute-start(f32[16,128]{1,0:T(8,128)S(1)} %add_add_fusion.1), channel_id=1, source_target_pairs={{0,128},{32,160},{64,192},{96,224},{128,0},{160,32},{192,64},{224,... | collective-permute-start | bytes 24584 | tf_op jit(solution)/shard_map/ppermute | solution.py:307
  91.6 7.3 %collective-permute-start.31 = (f32[16,128]{1,0:T(8,128)S(1)}, f32[16,128]{1,0:T(8,128)S(1)}, u32[]{:S(2)}, u32[]{:S(2)}) collective-permute-start(f32[16,128]{1,0:T(8,128)S(1)} %add_add_fusion.1), channel_id=1, source_target_pairs={{0,64},{32,96},{64,0},{96,32},{128,192},{160,224},{192,128},{224,1... | collective-permute-start | bytes 24584 | tf_op jit(solution)/shard_map/ppermute | solution.py:307
  (4 other events, 43.9 us)
